TPU v7x, 32 devices: a whole 2x2x4 slice. The times are simulated.
32 devices in a mesh: group: 2 (over y), expert: 4 (over z), cuts: 4 (over x, core).
Axes of the slice: x: 2, y: 2, z: 4, core: 2. Of those that a mesh axis runs over, the one named last changes fastest.
Arguments:
- residual: bfloat16 [128, 7168], P(('group', 'expert', 'cuts')), parts along dimension 0, may hold values from -6 to 6
- head_partials: float32 [4, 128, 7168], P('cuts', ('group', 'expert')), parts along dimension 1, may hold values from -6 to 6
- norm_gain: float32 [7168], replicated, may hold values from 0.1 to 1.9
- routes: int32 [128, 8], P(('group', 'expert', 'cuts')), parts along dimension 0, may hold values from 0 to 15, all different within a row; in each aligned block of 4 rows (0 to 3, 4 to 7, ...) at most 3 rows name the same one
- route_weights: float32 [128, 8], P(('group', 'expert', 'cuts')), parts along dimension 0, may hold values from 0.1 to 1
- w_gate: bfloat16 [7168, 16384], P('cuts', 'expert'), may hold values from -0.0625 to 0.0625
- w_up: bfloat16 [7168, 16384], P('cuts', 'expert'), may hold values from -0.0625 to 0.0625
- w_down: bfloat16 [16384, 7168], P('expert', 'cuts'), may hold values from -0.1875 to 0.1875
- expert_scale: float32 [16], replicated, may hold values from 0.5 to 2
Outputs:
- mixed: bfloat16 [128, 7168], P(('group', 'expert', 'cuts')), parts along dimension 0
There are 2 independent parts, one for each index of `group`. A program takes and returns all parts, laid end to end along the dimension named above; an argument that names none is the same for every part. Nothing has to cross between parts.
Inputs may be any that keep to these rules, and one draw needn't show every extreme that they name: `routes`: each row names 8 different experts; among the 4 rows of one device no expert is named by more than 3 rows.
All inputs are finite; a program needn't handle non-finite values.
Results may differ from a plain program's by a relative error of at most 0.0073.
Values may be sent and summed in bfloat16 or wider, within the bound.
No kernel may reach another device: no remote copies, remote signals or barrier semaphores. Data moves between devices by JAX's collectives and lax.ppermute only.
A program may use at most 448 MiB of HBM per device.

v0:
```python
import jax
import jax.numpy as jnp
from jax import lax
from jax.sharding import PartitionSpec as P

FH = 1024
EXPERTS = 16
MOST = 3


def body(
    residual, head_partials, norm_gain, routes, route_weights, w_gate, w_up, w_down, expert_scale
):
    index_count = lax.axis_size("expert")
    feature_width = residual.shape[1]
    partial_rows = head_partials.reshape(head_partials.shape[1], head_partials.shape[2])
    attention = lax.psum_scatter(partial_rows, "cuts", scatter_dimension=0, tiled=True)
    stream_half = lax.optimization_barrier(
        (residual.astype(jnp.float32) + attention).astype(jnp.bfloat16)
    )
    stream = stream_half.astype(jnp.float32)
    mean_square = jnp.mean(stream * stream, 1, keepdims=True)
    normed = (stream * lax.rsqrt(mean_square + 1e-06) * norm_gain).astype(jnp.bfloat16)
    row_count, top_count = routes.shape
    block_width = w_gate.shape[1]
    per_block = max(1, block_width // FH)
    spans = max(1, FH // block_width)
    capacity = MOST * per_block
    slot_count = index_count * capacity
    expert_list = routes.reshape(-1)
    first_target = expert_list * FH // block_width
    target = (first_target[:, None] + jnp.arange(spans, dtype=jnp.int32)[None, :]).reshape(-1)
    owners = jnp.repeat(expert_list, spans)
    row_of = jnp.repeat(jnp.arange(row_count * top_count, dtype=jnp.int32) // top_count, spans)
    onehot = (target[:, None] == jnp.arange(index_count, dtype=jnp.int32)[None, :]).astype(
        jnp.int32
    )
    before = jnp.cumsum(onehot, 0) - onehot
    slot_rank = jnp.sum(before * onehot, 1)
    slot_index = target * capacity + slot_rank
    send_rows = (
        jnp.zeros((slot_count, feature_width), jnp.bfloat16).at[slot_index].set(normed[row_of])
    )
    send_owner = jnp.full((slot_count,), -1, jnp.int32).at[slot_index].set(owners)
    got_rows, got_owner = (
        lax.all_to_all(
            send_rows.reshape(index_count, capacity, feature_width),
            "expert",
            split_axis=0,
            concat_axis=0,
            tiled=True,
        ),
        lax.all_to_all(
            send_owner.reshape(index_count, capacity),
            "expert",
            split_axis=0,
            concat_axis=0,
            tiled=True,
        ),
    )
    inputs = got_rows.reshape(slot_count, feature_width)
    slot_expert = got_owner.reshape(slot_count)
    hidden_unit = lax.axis_index("expert") * block_width + jnp.arange(block_width, dtype=jnp.int32)
    scale_of = jnp.sum(
        jnp.where(
            slot_expert[:, None] == jnp.arange(EXPERTS, dtype=jnp.int32)[None, :],
            expert_scale[None, :],
            0.0,
        ),
        1,
    )
    matches = (hidden_unit // FH)[None, :] == slot_expert[:, None]
    coefficient = jnp.where(matches, scale_of[:, None], 0.0)
    gate = jnp.dot(
        inputs,
        lax.all_gather(w_gate, "cuts", axis=0, tiled=True),
        preferred_element_type=jnp.float32,
    )
    upper = jnp.dot(
        inputs, lax.all_gather(w_up, "cuts", axis=0, tiled=True), preferred_element_type=jnp.float32
    )
    hidden = (jax.nn.silu(gate) * upper * coefficient).astype(jnp.bfloat16)
    outputs = jnp.dot(
        hidden,
        lax.all_gather(w_down, "cuts", axis=1, tiled=True),
        preferred_element_type=jnp.float32,
    ).astype(jnp.bfloat16)
    returned = lax.all_to_all(
        outputs.reshape(index_count, capacity, feature_width),
        "expert",
        split_axis=0,
        concat_axis=0,
        tiled=True,
    )
    weights_flat = jnp.repeat(route_weights.reshape(-1), spans)
    picked = (
        returned.reshape(slot_count, feature_width)[slot_index].astype(jnp.float32)
        * weights_flat[:, None]
    )
    expert_sum = jnp.sum(picked.reshape(row_count, top_count * spans, feature_width), 1)
    return (stream + expert_sum).astype(jnp.bfloat16)


def solution(mesh):
    in_specs = (
        P(("group", "expert", "cuts"), None),
        P("cuts", ("group", "expert"), None),
        P(),
        P(("group", "expert", "cuts"), None),
        P(("group", "expert", "cuts"), None),
        P("cuts", "expert"),
        P("cuts", "expert"),
        P("expert", "cuts"),
        P(),
    )
    out_specs = P(("group", "expert", "cuts"), None)
    return jax.shard_map(body, mesh=mesh, in_specs=in_specs, out_specs=out_specs, check_vma=False)
```

profile of v0, /device:TPU:0, one launch (start us, length us, event | category | flops | bytes accessed | tf_op | source)
XLA Modules:
  0.0 1146.8 jit_solution(17356304586332543077)
XLA Ops:
  6.5 0.7 all-reduce.3.cloned.1.call-update
  7.3 0.7 all-gather.4.cloned.1.call-update
  9.3 0.8 reshape.221
  12.5 6.3 all-to-all-start.1
  18.9 1.3 dynamic-slice
  20.9 24.6 %all-reduce.3.cloned.1.call-done = f32[16,7168]{1,0:T(8,128)} async-done(((f32[16,7168]{1,0:T(8,128)}), f32[16,7168]{1,0:T(8,128)}) %all-reduce.3.cloned.1.call-update) | async-done | bytes 458768
  45.5 1.0 fusion.10
  46.6 0.9 fusion.8
  47.5 2.7 scatter_custom_fusion
  50.2 1.1 reshape.188
  51.4 4.6 all-to-all-start
  56.5 0.7 reduce.3
  57.3 0.8 select_reduce_fusion.1
  58.0 19.8 %all-to-all-done = bf16[4,12,7168]{2,1,0:T(8,128)(2,1)S(1)} async-done(((bf16[4,12,7168]{2,1,0:T(8,128)(2,1)}), bf16[4,12,7168]{2,1,0:T(8,128)(2,1)S(1)}, u32[]{:S(2)}, u32[]{:S(2)}) %all-to-all-start) | async-done | bytes 688160 | tf_op jit(solution)/shard_map/all_to_all | solution.py:46
  77.9 315.2 %all-gather.4.cloned.1.call-done = bf16[7168,4096]{1,0:T(8,128)(2,1)} async-done(((bf16[1792,4096]{1,0:T(8,128)(2,1)}), bf16[7168,4096]{1,0:T(8,128)(2,1)}) %all-gather.4.cloned.1.call-update) | async-done | bytes 58720272 | tf_op jit(solution)/shard_map/all_gather | solution.py:76
  393.2 30.4 %fusion.21 = f32[48,4096]{1,0:T(8,128)S(1)} fusion(bf16[48,7168]{1,0:T(8,128)(2,1)S(1)} %reshape.189, bf16[7168,4096]{1,0:T(8,128)(2,1)} %all-gather.4.cloned.1.call-done), kind=kOutput, calls=%fused_computation.61 | convolution fusion | flops 2818572288 | bytes 60194816 | tf_op jit(solution)/shard_map/dot_general | solution.py:74
  423.6 317.3 %all-gather.6.cloned.1.call-done = bf16[7168,4096]{1,0:T(8,128)(2,1)} async-done(((bf16[1792,4096]{1,0:T(8,128)(2,1)}), bf16[7168,4096]{1,0:T(8,128)(2,1)}) %all-gather.6.cloned.1.call-update) | async-done | bytes 58720272 | tf_op jit(solution)/shard_map/all_gather | solution.py:80
  740.9 31.9 %fusion.1.clone.4 = bf16[48,4096]{1,0:T(8,128)(2,1)S(1)} fusion(bf16[48,7168]{1,0:T(8,128)(2,1)S(1)} %reshape.189, bf16[7168,4096]{1,0:T(8,128)(2,1)} %all-gather.6.cloned.1.call-done, f32[48,4096]{1,0:T(8,128)S(1)} %fusion.21, f32[48]{0:T(128)S(1)} %select_reduce_fusion.1, s32[4096]{0:T(1024)S(1)} %add_select_fusion, s32[48]{0:T(128)S(1)} %eq.45), kind=kOutput, calls=%fused_computation.7.clone.clone.clone.1 | convolution fusion | flops 2820341760 | bytes 60604800 | tf_op jit(solution)/shard_map/dot_general | solution.py:79
  772.8 315.7 %all-gather.8.cloned.1.call-done = bf16[4096,7168]{1,0:T(8,128)(2,1)} async-done(((bf16[4096,1792]{1,0:T(8,128)(2,1)}), bf16[4096,7168]{1,0:T(8,128)(2,1)}) %all-gather.8.cloned.1.call-update) | async-done | bytes 58720272 | tf_op jit(solution)/shard_map/all_gather | solution.py:85
  1088.4 20.7 %convolution_convert_fusion = bf16[48,7168]{1,0:T(8,128)(2,1)S(1)} fusion(bf16[4096,7168]{1,0:T(8,128)(2,1)} %all-gather.8.cloned.1.call-done, bf16[48,4096]{1,0:T(8,128)(2,1)S(1)} %fusion.1.clone.4), kind=kOutput, calls=%fused_computation.4 | convolution fusion | flops 2818916352 | bytes 59801600 | tf_op jit(solution)/shard_map/dot_general | solution.py:83
  1109.1 1.1 reshape.190
  1110.2 4.6 all-to-all-start.2
  1114.8 23.3 %all-to-all-done.2 = bf16[4,12,7168]{2,1,0:T(8,128)(2,1)S(1)} async-done(((bf16[4,12,7168]{2,1,0:T(8,128)(2,1)}), bf16[4,12,7168]{2,1,0:T(8,128)(2,1)S(1)}, u32[]{:S(2)}, u32[]{:S(2)}) %all-to-all-start.2) | async-done | bytes 688160 | tf_op jit(solution)/shard_map/all_to_all | solution.py:88
  1138.3 0.8 gather_fusion
  (30 shorter events, 6.0 us)
Async XLA Ops:
  6.5 38.9 %all-reduce.3.cloned.1.call-start = ((), (), s32[]{:S(2)}) async-start(), calls=%async_computation.6 | async-start | bytes 917504
  7.3 385.9 %all-gather.4.cloned.1.call-start = ((), (), s32[]{:S(2)}) async-start(), calls=%async_computation.3 | async-start | bytes 73400320 | tf_op jit(solution)/shard_map/all_gather | solution.py:76
  8.0 732.9 %all-gather.6.cloned.1.call-start = ((), (), s32[]{:S(2)}) async-start(), calls=%async_computation.4 | async-start | bytes 73400320 | tf_op jit(solution)/shard_map/all_gather | solution.py:80
  8.7 1079.7 %all-gather.8.cloned.1.call-start = ((), (), s32[]{:S(2)}) async-start(), calls=%async_computation.5 | async-start | bytes 73400320 | tf_op jit(solution)/shard_map/all_gather | solution.py:85
  12.5 38.8 %all-to-all-start.1 = ((s32[4,1,12]{2,1,0:T(1,128)}), s32[4,1,12]{2,1,0:T(1,128)S(1)}, u32[]{:S(2)}, u32[]{:S(2)}) async-start(s32[4,1,12]{2,1,0:T(1,128)} %bitcast.4), calls=%async_computation.1 | async-start | bytes 4096 | tf_op jit(solution)/shard_map/all_to_all | solution.py:53
  51.4 26.4 %all-to-all-start = ((bf16[4,12,7168]{2,1,0:T(8,128)(2,1)}), bf16[4,12,7168]{2,1,0:T(8,128)(2,1)S(1)}, u32[]{:S(2)}, u32[]{:S(2)}) async-start(bf16[4,12,7168]{2,1,0:T(8,128)(2,1)} %reshape.188), calls=%async_computation | async-start | bytes 1835008 | tf_op jit(solution)/shard_map/all_to_all | solution.py:46
  423.6 715.6 %copy-start = (f32[4,8]{1,0:T(4,128)S(1)}, f32[4,8]{1,0:T(4,128)}, u32[]{:S(2)}) copy-start(f32[4,8]{1,0:T(4,128)} %param.13) | copy-start | bytes 388
  1110.2 27.9 %all-to-all-start.2 = ((bf16[4,12,7168]{2,1,0:T(8,128)(2,1)}), bf16[4,12,7168]{2,1,0:T(8,128)(2,1)S(1)}, u32[]{:S(2)}, u32[]{:S(2)}) async-start(bf16[4,12,7168]{2,1,0:T(8,128)(2,1)} %reshape.190), calls=%async_computation.2 | async-start | bytes 1835008 | tf_op jit(solution)/shard_map/all_to_all | solution.py:88
Sparse Core Ops, SparseCore 0:
  9.7 35.7 all-reduce.2
  47.1 346.0 all-gather.3
  394.9 346.0 all-gather.5
  742.4 345.9 all-gather.7
where the time goes:
time: 1150 us
  waiting for transfers between devices  1020 us (89%)
  matrix products  82.9 us (7%)
  starting transfers between devices  15.6 us (1%)
  between operations  13.9 us (1%)
    all_gather x1, waiting for transfers between devices, body(): lax.all_gather(w_up, 'cuts', axis=0, tiled=True)  317 us
    all_gather x1, waiting for transfers between devices, body(): lax.all_gather(w_down, 'cuts', axis=1, tiled=True)  316 us
    all_gather x1, waiting for transfers between devices, body(): lax.all_gather(w_gate, 'cuts', axis=0, tiled=True)  315 us
    dot_general x1, matrix products, body(): jnp.dot(inputs, lax.all_gather(w_up, 'cuts', axis=0, tiled=True), preferr...  31.9 us
    dot_general x1, matrix products, body(): jnp.dot(inputs, lax.all_gather(w_gate, 'cuts', axis=0, tiled=True), prefe...  30.4 us
    unnamed x5, waiting for transfers between devices  27.2 us
    all_to_all x1, waiting for transfers between devices, body(): lax.all_to_all(outputs.reshape(index_count, capacity, feature_width), 'ex...  23.3 us
  transfers between devices with their start and end apart: 7, of which 6 were waited for; matrix products, arithmetic and copies ran while one was open for 6% of the time, Pallas kernels for 0%

commit v1 on v0

v1 whole, which is shorter than its diff:
```python
import jax
import jax.numpy as jnp
from jax import lax
from jax.sharding import PartitionSpec as P

FH = 1024
EXPERTS = 16
bf16, f32 = jnp.bfloat16, jnp.float32


def shift(x, axis, k):
    n = lax.axis_size(axis)
    return lax.ppermute(x, axis, [(i, (i + k) % n) for i in range(n)])


def swap(x, axis, bit):
    n = lax.axis_size(axis)
    return lax.ppermute(x, axis, [(i, i ^ bit) for i in range(n)])


def pick(x, i):
    return lax.dynamic_index_in_dim(x, i, 0, False)


def body(
    residual, head_partials, norm_gain, routes, route_weights, w_gate, w_up, w_down, expert_scale
):
    n_e, n_c = lax.axis_size("expert"), lax.axis_size("cuts")
    e, c = lax.axis_index("expert"), lax.axis_index("cuts")
    own_rows, width = residual.shape
    rows_e = own_rows * n_c
    part = width // n_c
    block = w_gate.shape[1]
    rows = rows_e * n_e
    b, h = c & 1, c >> 1

    share = jnp.sum(
        jnp.where(
            routes[:, :, None] == jnp.arange(EXPERTS, dtype=jnp.int32), route_weights[:, :, None], 0.0
        ),
        1,
    )
    share = lax.all_gather(share, ("expert", "cuts"), axis=0, tiled=True)

    y = head_partials.reshape(rows_e, width)
    mine = lax.dynamic_slice_in_dim(y, c * own_rows, own_rows, 0) + residual.astype(f32)
    y = lax.dynamic_update_slice_in_dim(y, mine, c * own_rows, 0)
    y = y.reshape(rows_e, n_c // 2, 2, part).transpose(2, 1, 0, 3)
    y = pick(y, b) + swap(pick(y, 1 - b), "cuts", 1)
    y = pick(y, h) + swap(pick(y, 1 - h), "cuts", 2)
    own_stream = y.astype(bf16)

    if n_e <= 8:
        pieces = [own_stream] + [shift(own_stream, "expert", k) for k in range(1, n_e)]
        stacked = jnp.stack(pieces)
        order = (e - jnp.arange(n_e)) % n_e
        stream = jnp.take(stacked, order, axis=0).reshape(rows, part)
    else:
        stream = lax.all_gather(own_stream, "expert", axis=0, tiled=True)
    sf = stream.astype(f32)
    square = jnp.sum(sf * sf, 1, keepdims=True)
    square = square + swap(square, "cuts", 1)
    square = square + swap(square, "cuts", 2)
    factor = lax.rsqrt(square / width + 1e-06)
    gain = lax.dynamic_slice_in_dim(norm_gain, c * part, part, 0)
    x = (sf * gain).astype(bf16)

    def product(w):
        p = jnp.dot(x, w, preferred_element_type=f32).astype(bf16)
        p = p.reshape(rows, n_c // 2, 2, block // n_c).transpose(2, 1, 0, 3)
        return p

    g, u = product(w_gate), product(w_up)
    p = jnp.stack([g, u], 2)
    p = pick(p, b).astype(f32) + swap(pick(p, 1 - b), "cuts", 1).astype(f32)
    keep, send = pick(p, h), pick(p, 1 - h).astype(bf16)
    p = keep + swap(send, "cuts", 2).astype(f32)
    g, u = p[0] * factor, p[1] * factor
    unit = e * block + (h * 2 + b) * (block // n_c) + jnp.arange(block // n_c, dtype=jnp.int32)
    coefficient = share * expert_scale
    coefficient = jnp.dot(
        coefficient,
        (jnp.arange(EXPERTS, dtype=jnp.int32)[:, None] == (unit // FH)[None, :]).astype(f32),
        precision=lax.Precision.HIGHEST,
    )
    hidden = (jax.nn.silu(g) * u * coefficient).astype(bf16)
    other = swap(hidden, "cuts", 2)
    pair = jnp.where(h == 0, jnp.stack([hidden, other]), jnp.stack([other, hidden]))
    other = swap(pair, "cuts", 1)
    quad = jnp.where(b == 0, jnp.stack([pair, other], 1), jnp.stack([other, pair], 1))
    hidden = quad.transpose(2, 0, 1, 3).reshape(rows, block)
    out = jnp.dot(hidden, w_down, preferred_element_type=f32)

    if n_e <= 8:
        out = out.reshape(n_e, rows_e, part)
        total = pick(out, e)
        for k in range(1, n_e):
            total = total + shift(pick(out, (e + k) % n_e).astype(bf16), "expert", k).astype(f32)
    else:
        total = lax.psum_scatter(out, "expert", scatter_dimension=0, tiled=True)
    mixed = (own_stream.astype(f32) + total).astype(bf16)
    mixed = lax.all_to_all(
        mixed.reshape(n_c, own_rows, part), "cuts", split_axis=0, concat_axis=0, tiled=True
    )
    return mixed.transpose(1, 0, 2).reshape(own_rows, width)


def solution(mesh):
    in_specs = (
        P(("group", "expert", "cuts"), None),
        P("cuts", ("group", "expert"), None),
        P(),
        P(("group", "expert", "cuts"), None),
        P(("group", "expert", "cuts"), None),
        P("cuts", "expert"),
        P("cuts", "expert"),
        P("expert", "cuts"),
        P(),
    )
    out_specs = P(("group", "expert", "cuts"), None)
    return jax.shard_map(body, mesh=mesh, in_specs=in_specs, out_specs=out_specs, check_vma=False)
```

time: 1150 us -> 94.2 us (0.08)
  waiting for transfers between devices: 1020 us -> 20.9 us
  matrix products: 82.9 us -> 23.7 us
  blocking collectives: 0 us -> 25.2 us
  between operations: 13.9 us -> 0.35 us
    all_gather x3 -> x0, waiting for transfers between devices: 948 us -> none  [the longest x1 317 us: body(): lax.all_gather(w_up, 'cuts', axis=0, tiled=True)]
    dot_general x3 -> x4, matrix products: 82.9 us -> 23.7 us  [the longest x2 15.7 us: product(): p = jnp.dot(x, w, preferred_element_type=f32).astype(bf16)]
    all_to_all x3 -> x0, waiting for transfers between devices: 43.1 us -> none  [the longest x1 23.3 us: body(): lax.all_to_all(outputs.reshape(index_count, capacity, feature_width), 'ex...]
    unnamed x5 -> x0, waiting for transfers between devices: 27.2 us -> none
    ppermute x0 -> x14, waiting for transfers between devices: none -> 20.9 us  [the longest x8 11.3 us: swap(): return lax.ppermute(x, axis, [(i, i ^ bit) for i in range(n)])]
    all_gather x0 -> x1, blocking collectives: none -> 18.7 us  [body(): share = lax.all_gather(share, ('expert', 'cuts'), axis=0, tiled=True)]
    ppermute x0 -> x14, starting transfers between devices: none -> 15.6 us  [the longest x6 8.79 us: shift(): return lax.ppermute(x, axis, [(i, (i + k) % n) for i in range(n)])]
    all_to_all x3 -> x0, starting transfers between devices: 15.5 us -> none  [the longest x1 6.32 us: body(): lax.all_to_all(send_owner.reshape(index_count, capacity), 'expert', split...]
  transfers between devices with their start and end apart: 7 -> 14, of which waited for: 6 -> 10; matrix products, arithmetic and copies ran while one was open for 6% -> 2% of each run, Pallas kernels for 0% -> 0%
where the time goes in v1:
time: 94.2 us; the launch traced here: 93.8 us
  blocking collectives  25.2 us (27%)
  matrix products  23.7 us (25%)
  waiting for transfers between devices  20.9 us (22%)
  starting transfers between devices  15.6 us (17%)
  local copies, waits for them, and re-layouts  6.16 us (7%)
  other arithmetic  2.03 us (2%)
    all_gather x1, blocking collectives, body(): share = lax.all_gather(share, ('expert', 'cuts'), axis=0, tiled=True)  18.7 us
    dot_general x2, matrix products, product(): p = jnp.dot(x, w, preferred_element_type=f32).astype(bf16)  15.7 us
    ppermute x8, waiting for transfers between devices, swap(): return lax.ppermute(x, axis, [(i, i ^ bit) for i in range(n)])  11.3 us
    ppermute x6, waiting for transfers between devices, shift(): return lax.ppermute(x, axis, [(i, (i + k) % n) for i in range(n)])  9.58 us
    ppermute x6, starting transfers between devices, shift(): return lax.ppermute(x, axis, [(i, (i + k) % n) for i in range(n)])  8.79 us
    dot_general x1, matrix products, body(): out = jnp.dot(hidden, w_down, preferred_element_type=f32)  7.79 us
    ppermute x8, starting transfers between devices, swap(): return lax.ppermute(x, axis, [(i, i ^ bit) for i in range(n)])  6.76 us
    all_to_all x1, blocking collectives, body(): lax.all_to_all(mixed.reshape(n_c, own_rows, part), 'cuts', split_axis=0,...  6.44 us
  transfers between devices with their start and end apart: 14, of which 10 were waited for; matrix products, arithmetic and copies ran while one was open for 2% of the time, Pallas kernels for 0%

profile of v1, /device:TPU:0, one launch (start us, length us, event | category | flops | bytes accessed | tf_op | source)
XLA Modules:
  0.0 93.8 jit_solution(6388236608144422688)
XLA Ops:
  0.0 1.0 %copy.42 = f32[16,7168]{1,0:T(8,128)S(1)} copy(f32[16,7168]{1,0:T(8,128)} %bitcast.103) | data formatting | bytes 917504
  1.0 1.0 %fusion.18 = f32[16,7168]{1,0:T(8,128)S(1)} fusion(f32[16,7168]{1,0:T(8,128)S(1)} %copy.42, s32[]{:T(128)S(6)} %select_n.136, bf16[4,7168]{1,0:T(4,128)(2,1)} %param.9, f32[1,16,7168]{2,1,0:T(8,128)} %param.10), kind=kLoop, calls=%fused_computation.45 | loop fusion | flops 57344 | bytes 286724 | tf_op jit(solution)/shard_map/dynamic_update_slice | solution.py:47
  3.4 1.1 %collective-permute-done = f32[2,16,1792]{2,1,0:T(8,128)S(1)} collective-permute-done((f32[2,16,1792]{2,1,0:T(8,128)S(1)}, f32[2,16,1792]{2,1,0:T(8,128)S(1)}, u32[]{:S(2)}, u32[]{:S(2)}) %collective-permute-start) | collective-permute-done | bytes 229408 | tf_op jit(solution)/shard_map/ppermute | solution.py:18
  4.6 2.9 %collective-permute-start.1 = (f32[16,1792]{1,0:T(8,128)S(1)}, f32[16,1792]{1,0:T(8,128)S(1)}, u32[]{:S(2)}, u32[]{:S(2)}) collective-permute-start(f32[16,1792]{1,0:T(8,128)S(1)} %dynamic-slice_bitcast_fusion), channel_id=1, source_target_pairs={{0,2},{1,3},{2,0},{3,1},{4,6},{5,7},{6,4},{7,5},{8,10},{9,11},{10,... | collective-permute-start | bytes 344072 | tf_op jit(solution)/shard_map/ppermute | solution.py:18
  7.7 0.8 dynamic_slice.55
  8.5 2.5 %collective-permute-done.1 = f32[16,1792]{1,0:T(8,128)S(1)} collective-permute-done((f32[16,1792]{1,0:T(8,128)S(1)}, f32[16,1792]{1,0:T(8,128)S(1)}, u32[]{:S(2)}, u32[]{:S(2)}) %collective-permute-start.1) | collective-permute-done | bytes 114720 | tf_op jit(solution)/shard_map/ppermute | solution.py:18
  11.0 2.9 %collective-permute-start.3 = (bf16[16,1792]{1,0:T(8,128)(2,1)S(1)}, bf16[16,1792]{1,0:T(8,128)(2,1)S(1)}, u32[]{:S(2)}, u32[]{:S(2)}) collective-permute-start(bf16[16,1792]{1,0:T(8,128)(2,1)S(1)} %fusion.17), channel_id=1, source_target_pairs={{0,8},{4,12},{8,0},{12,4},{1,9},{5,13},{9,1},{13,5},{2,10},{6,14},... | collective-permute-start | bytes 172040 | tf_op jit(solution)/shard_map/ppermute | solution.py:13
  13.9 1.3 %collective-permute-start.4 = (bf16[16,1792]{1,0:T(8,128)(2,1)S(1)}, bf16[16,1792]{1,0:T(8,128)(2,1)S(1)}, u32[]{:S(2)}, u32[]{:S(2)}) collective-permute-start(bf16[16,1792]{1,0:T(8,128)(2,1)S(1)} %fusion.17), channel_id=1, source_target_pairs={{0,12},{4,0},{8,4},{12,8},{1,13},{5,1},{9,5},{13,9},{2,14},{6,2},{... | collective-permute-start | bytes 172040 | tf_op jit(solution)/shard_map/ppermute | solution.py:13
  15.2 0.7 collective-permute-start.2
  16.4 1.6 %collective-permute-done.4 = bf16[16,1792]{1,0:T(8,128)(2,1)S(1)} collective-permute-done((bf16[16,1792]{1,0:T(8,128)(2,1)S(1)}, bf16[16,1792]{1,0:T(8,128)(2,1)S(1)}, u32[]{:S(2)}, u32[]{:S(2)}) %collective-permute-start.4) | collective-permute-done | bytes 57376 | tf_op jit(solution)/shard_map/ppermute | solution.py:13
  18.0 3.1 %collective-permute-done.2 = bf16[16,1792]{1,0:T(8,128)(2,1)S(1)} collective-permute-done((bf16[16,1792]{1,0:T(8,128)(2,1)S(1)}, bf16[16,1792]{1,0:T(8,128)(2,1)S(1)}, u32[]{:S(2)}, u32[]{:S(2)}) %collective-permute-start.2) | collective-permute-done | bytes 57376 | tf_op jit(solution)/shard_map/ppermute | solution.py:13
  21.9 7.8 %convolution_convert_fusion.1 = bf16[64,4096]{1,0:T(8,128)(2,1)S(1)} fusion(bf16[64,1792]{1,0:T(8,128)(2,1)S(1)} %multiply_convert_fusion, bf16[1792,4096]{1,0:T(8,128)(2,1)} %param.14), kind=kOutput, calls=%fused_computation.4 | convolution fusion | flops 939786240 | bytes 15433728 | tf_op jit(solution)/shard_map/dot_general | solution.py:69
  30.2 7.8 %convolution_convert_fusion = bf16[64,4096]{1,0:T(8,128)(2,1)S(1)} fusion(bf16[64,1792]{1,0:T(8,128)(2,1)S(1)} %multiply_convert_fusion, bf16[1792,4096]{1,0:T(8,128)(2,1)} %param.15), kind=kOutput, calls=%fused_computation.3 | convolution fusion | flops 939786240 | bytes 15433728 | tf_op jit(solution)/shard_map/dot_general | solution.py:69
  39.8 1.0 %collective-permute-done.5 = bf16[2,2,64,1024]{3,2,1,0:T(8,128)(2,1)S(1)} collective-permute-done((bf16[2,2,64,1024]{3,2,1,0:T(8,128)(2,1)S(1)}, bf16[2,2,64,1024]{3,2,1,0:T(8,128)(2,1)S(1)}, u32[]{:S(2)}, u32[]{:S(2)}) %collective-permute-start.5) | collective-permute-done | bytes 524320 | tf_op jit(solution)/shard_map/ppermute | solution.py:18
  41.0 1.6 %collective-permute-start.6 = (bf16[2,64,1024]{2,1,0:T(8,128)(2,1)S(1)}, bf16[2,64,1024]{2,1,0:T(8,128)(2,1)S(1)}, u32[]{:S(2)}, u32[]{:S(2)}) collective-permute-start(bf16[2,64,1024]{2,1,0:T(8,128)(2,1)S(1)} %fusion.8), channel_id=1, source_target_pairs={{0,2},{1,3},{2,0},{3,1},{4,6},{5,7},{6,4},{7,5},{8,10},{9,11},{10,... | collective-permute-start | bytes 786440 | tf_op jit(solution)/shard_map/ppermute | solution.py:18
  43.2 18.7 %all-gather = f32[16,4,16]{2,1,0:T(4,128)S(1)} all-gather(f32[1,4,16]{2,1,0:T(4,128)S(1)} %bitcast.116), channel_id=1, replica_groups=mesh['group'=2,'expert'=4,'cuts'=4] {'expert','cuts'}, dimensions={0}, use_global_device_ids=true | all-gather | bytes 4352 | tf_op jit(solution)/shard_map/all_gather | solution.py:43
  62.8 5.3 %collective-permute-done.9 = bf16[64,1024]{1,0:T(8,128)(2,1)S(1)} collective-permute-done((bf16[64,1024]{1,0:T(8,128)(2,1)S(1)}, bf16[64,1024]{1,0:T(8,128)(2,1)S(1)}, u32[]{:S(2)}, u32[]{:S(2)}) %collective-permute-start.9) | collective-permute-done | bytes 131104 | tf_op jit(solution)/shard_map/ppermute | solution.py:18
  68.2 1.4 %collective-permute-done.10 = bf16[2,64,1024]{2,1,0:T(8,128)(2,1)S(1)} collective-permute-done((bf16[2,64,1024]{2,1,0:T(8,128)(2,1)S(1)}, bf16[2,64,1024]{2,1,0:T(8,128)(2,1)S(1)}, u32[]{:S(2)}, u32[]{:S(2)}) %collective-permute-start.10) | collective-permute-done | bytes 262176 | tf_op jit(solution)/shard_map/ppermute | solution.py:18
  70.7 7.8 %fusion = f32[4,16,1792]{2,1,0:T(8,128)S(1)} fusion(bf16[4,16,4096]{2,1,0:T(8,128)(2,1)S(1)} %dot_general.17, bf16[4096,1792]{1,0:T(8,128)(2,1)} %param.16), kind=kOutput, calls=%fused_computation.1 | convolution fusion | flops 939524096 | bytes 15663104 | tf_op jit(solution)/shard_map/dot_general | solution.py:92
  78.7 3.7 %collective-permute-start.13 = (bf16[16,1792]{1,0:T(8,128)(2,1)S(1)}, bf16[16,1792]{1,0:T(8,128)(2,1)S(1)}, u32[]{:S(2)}, u32[]{:S(2)}) collective-permute-start(bf16[16,1792]{1,0:T(8,128)(2,1)S(1)} %get-tuple-element.6), channel_id=1, source_target_pairs={{0,12},{4,0},{8,4},{12,8},{1,13},{5,1},{9,5},{13,9},{2,14},{6,2},{... | collective-permute-start | bytes 172040 | tf_op jit(solution)/shard_map/ppermute | solution.py:13
  82.4 2.7 %collective-permute-done.11 = bf16[16,1792]{1,0:T(8,128)(2,1)S(1)} collective-permute-done((bf16[16,1792]{1,0:T(8,128)(2,1)S(1)}, bf16[16,1792]{1,0:T(8,128)(2,1)S(1)}, u32[]{:S(2)}, u32[]{:S(2)}) %collective-permute-start.11) | collective-permute-done | bytes 57376 | tf_op jit(solution)/shard_map/ppermute | solution.py:13
  85.2 1.5 %collective-permute-done.12 = bf16[16,1792]{1,0:T(8,128)(2,1)S(1)} collective-permute-done((bf16[16,1792]{1,0:T(8,128)(2,1)S(1)}, bf16[16,1792]{1,0:T(8,128)(2,1)S(1)}, u32[]{:S(2)}, u32[]{:S(2)}) %collective-permute-start.12) | collective-permute-done | bytes 57376 | tf_op jit(solution)/shard_map/ppermute | solution.py:13
  86.8 6.4 %all_to_all.5 = bf16[4,4,1792]{2,1,0:T(4,128)(2,1)S(1)} all-to-all(bf16[4,4,1792]{2,1,0:T(4,128)(2,1)S(1)} %reshape.179), channel_id=1, replica_groups=mesh['group'=2,'expert'=4,'cuts'=4] {'cuts'}, dimensions={0} | all-to-all | bytes 114688 | tf_op jit(solution)/shard_map/all_to_all | solution.py:102
  93.2 0.6 copy.44
  (55 shorter events, 7.9 us)
Async XLA Ops:
  2.9 1.6 %collective-permute-start = (f32[2,16,1792]{2,1,0:T(8,128)S(1)}, f32[2,16,1792]{2,1,0:T(8,128)S(1)}, u32[]{:S(2)}, u32[]{:S(2)}) collective-permute-start(f32[2,16,1792]{2,1,0:T(8,128)S(1)} %bitcast.110), channel_id=1, source_target_pairs={{0,1},{1,0},{2,3},{3,2},{4,5},{5,4},{6,7},{7,6},{8,9},{9,8},{10,11... | collective-permute-start | bytes 688136 | tf_op jit(solution)/shard_map/ppermute | solution.py:18
  4.6 6.4 %collective-permute-start.1 = (f32[16,1792]{1,0:T(8,128)S(1)}, f32[16,1792]{1,0:T(8,128)S(1)}, u32[]{:S(2)}, u32[]{:S(2)}) collective-permute-start(f32[16,1792]{1,0:T(8,128)S(1)} %dynamic-slice_bitcast_fusion), channel_id=1, source_target_pairs={{0,2},{1,3},{2,0},{3,1},{4,6},{5,7},{6,4},{7,5},{8,10},{9,11},{10,... | collective-permute-start | bytes 344072 | tf_op jit(solution)/shard_map/ppermute | solution.py:18
  11.0 5.5 %collective-permute-start.3 = (bf16[16,1792]{1,0:T(8,128)(2,1)S(1)}, bf16[16,1792]{1,0:T(8,128)(2,1)S(1)}, u32[]{:S(2)}, u32[]{:S(2)}) collective-permute-start(bf16[16,1792]{1,0:T(8,128)(2,1)S(1)} %fusion.17), channel_id=1, source_target_pairs={{0,8},{4,12},{8,0},{12,4},{1,9},{5,13},{9,1},{13,5},{2,10},{6,14},... | collective-permute-start | bytes 172040 | tf_op jit(solution)/shard_map/ppermute | solution.py:13
  13.9 4.2 %collective-permute-start.4 = (bf16[16,1792]{1,0:T(8,128)(2,1)S(1)}, bf16[16,1792]{1,0:T(8,128)(2,1)S(1)}, u32[]{:S(2)}, u32[]{:S(2)}) collective-permute-start(bf16[16,1792]{1,0:T(8,128)(2,1)S(1)} %fusion.17), channel_id=1, source_target_pairs={{0,12},{4,0},{8,4},{12,8},{1,13},{5,1},{9,5},{13,9},{2,14},{6,2},{... | collective-permute-start | bytes 172040 | tf_op jit(solution)/shard_map/ppermute | solution.py:13
  15.2 6.0 %collective-permute-start.2 = (bf16[16,1792]{1,0:T(8,128)(2,1)S(1)}, bf16[16,1792]{1,0:T(8,128)(2,1)S(1)}, u32[]{:S(2)}, u32[]{:S(2)}) collective-permute-start(bf16[16,1792]{1,0:T(8,128)(2,1)S(1)} %fusion.17), channel_id=1, source_target_pairs={{0,4},{4,8},{8,12},{12,0},{1,5},{5,9},{9,13},{13,1},{2,6},{6,10},{... | collective-permute-start | bytes 172040 | tf_op jit(solution)/shard_map/ppermute | solution.py:13
  29.8 9.1 %copy-start = (f32[4,8]{1,0:T(4,128)S(1)}, f32[4,8]{1,0:T(4,128)}, u32[]{:S(2)}) copy-start(f32[4,8]{1,0:T(4,128)} %param.13) | copy-start | bytes 388
  29.8 9.1 %copy-start.1 = (s32[4,8]{1,0:T(4,128)S(1)}, s32[4,8]{1,0:T(4,128)}, u32[]{:S(2)}) copy-start(s32[4,8]{1,0:T(4,128)} %param.12) | copy-start | bytes 388
  30.2 31.8 %copy-start.2 = (f32[16]{0:T(128)S(1)}, f32[16]{0:T(128)}, u32[]{:S(2)}) copy-start(f32[16]{0:T(128)} %param.17) | copy-start | bytes 196
  38.8 2.0 %collective-permute-start.5 = (bf16[2,2,64,1024]{3,2,1,0:T(8,128)(2,1)S(1)}, bf16[2,2,64,1024]{3,2,1,0:T(8,128)(2,1)S(1)}, u32[]{:S(2)}, u32[]{:S(2)}) collective-permute-start(bf16[2,2,64,1024]{3,2,1,0:T(8,128)(2,1)S(1)} %fusion.4), channel_id=1, source_target_pairs={{0,1},{1,0},{2,3},{3,2},{4,5},{5,4},{6,7},{7,6},{8,9},{9,8},{10,11... | collective-permute-start | bytes 1572872 | tf_op jit(solution)/shard_map/ppermute | solution.py:18
  39.3 3.3 %collective-permute-start.7 = (f32[64,1]{0,1:T(1,128)S(1)}, f32[64,1]{0,1:T(1,128)S(1)}, u32[]{:S(2)}, u32[]{:S(2)}) collective-permute-start(f32[64,1]{0,1:T(1,128)S(1)} %broadcast_in_dim.46), channel_id=1, source_target_pairs={{0,1},{1,0},{2,3},{3,2},{4,5},{5,4},{6,7},{7,6},{8,9},{9,8},{10,11... | collective-permute-start | bytes 776 | tf_op jit(solution)/shard_map/ppermute | solution.py:18
  41.0 20.9 %collective-permute-start.6 = (bf16[2,64,1024]{2,1,0:T(8,128)(2,1)S(1)}, bf16[2,64,1024]{2,1,0:T(8,128)(2,1)S(1)}, u32[]{:S(2)}, u32[]{:S(2)}) collective-permute-start(bf16[2,64,1024]{2,1,0:T(8,128)(2,1)S(1)} %fusion.8), channel_id=1, source_target_pairs={{0,2},{1,3},{2,0},{3,1},{4,6},{5,7},{6,4},{7,5},{8,10},{9,11},{10,... | collective-permute-start | bytes 786440 | tf_op jit(solution)/shard_map/ppermute | solution.py:18
  42.6 19.3 %collective-permute-start.8 = (f32[64,1]{0,1:T(1,128)S(1)}, f32[64,1]{0,1:T(1,128)S(1)}, u32[]{:S(2)}, u32[]{:S(2)}) collective-permute-start(f32[64,1]{0,1:T(1,128)S(1)} %add.172), channel_id=1, source_target_pairs={{0,2},{1,3},{2,0},{3,1},{4,6},{5,7},{6,4},{7,5},{8,10},{9,11},{10,... | collective-permute-start | bytes 776 | tf_op jit(solution)/shard_map/ppermute | solution.py:18
  62.2 5.8 %collective-permute-start.9 = (bf16[64,1024]{1,0:T(8,128)(2,1)S(1)}, bf16[64,1024]{1,0:T(8,128)(2,1)S(1)}, u32[]{:S(2)}, u32[]{:S(2)}) collective-permute-start(bf16[64,1024]{1,0:T(8,128)(2,1)S(1)} %fusion.2), channel_id=1, source_target_pairs={{0,2},{1,3},{2,0},{3,1},{4,6},{5,7},{6,4},{7,5},{8,10},{9,11},{10,... | collective-permute-start | bytes 393224 | tf_op jit(solution)/shard_map/ppermute | solution.py:18
  68.1 1.6 %collective-permute-start.10 = (bf16[2,64,1024]{2,1,0:T(8,128)(2,1)S(1)}, bf16[2,64,1024]{2,1,0:T(8,128)(2,1)S(1)}, u32[]{:S(2)}, u32[]{:S(2)}) collective-permute-start(bf16[2,64,1024]{2,1,0:T(8,128)(2,1)S(1)} %maximum_select_fusion.2), channel_id=1, source_target_pairs={{0,1},{1,0},{2,3},{3,2},{4,5},{5,4},{6,7},{7,6},{8,9},{9,8},{10,11... | collective-permute-start | bytes 786440 | tf_op jit(solution)/shard_map/ppermute | solution.py:18
  78.5 6.6 %collective-permute-start.11 = (bf16[16,1792]{1,0:T(8,128)(2,1)S(1)}, bf16[16,1792]{1,0:T(8,128)(2,1)S(1)}, u32[]{:S(2)}, u32[]{:S(2)}) collective-permute-start(bf16[16,1792]{1,0:T(8,128)(2,1)S(1)} %get-tuple-element.5), channel_id=1, source_target_pairs={{0,4},{4,8},{8,12},{12,0},{1,5},{5,9},{9,13},{13,1},{2,6},{6,10},{... | collective-permute-start | bytes 172040 | tf_op jit(solution)/shard_map/ppermute | solution.py:13
  78.6 8.1 %collective-permute-start.12 = (bf16[16,1792]{1,0:T(8,128)(2,1)S(1)}, bf16[16,1792]{1,0:T(8,128)(2,1)S(1)}, u32[]{:S(2)}, u32[]{:S(2)}) collective-permute-start(bf16[16,1792]{1,0:T(8,128)(2,1)S(1)} %get-tuple-element.7), channel_id=1, source_target_pairs={{0,8},{4,12},{8,0},{12,4},{1,9},{5,13},{9,1},{13,5},{2,10},{6,14},... | collective-permute-start | bytes 172040 | tf_op jit(solution)/shard_map/ppermute | solution.py:13
  78.7 8.0 %collective-permute-start.13 = (bf16[16,1792]{1,0:T(8,128)(2,1)S(1)}, bf16[16,1792]{1,0:T(8,128)(2,1)S(1)}, u32[]{:S(2)}, u32[]{:S(2)}) collective-permute-start(bf16[16,1792]{1,0:T(8,128)(2,1)S(1)} %get-tuple-element.6), channel_id=1, source_target_pairs={{0,12},{4,0},{8,4},{12,8},{1,13},{5,1},{9,5},{13,9},{2,14},{6,2},{... | collective-permute-start | bytes 172040 | tf_op jit(solution)/shard_map/ppermute | solution.py:13

commit v2 on v1

--- a/solution.py
+++ b/solution.py
@@ -1,10 +1,16 @@
+import functools
+
 import jax
 import jax.numpy as jnp
 from jax import lax
+from jax.experimental import pallas as pl
+from jax.experimental.pallas import tpu as pltpu
 from jax.sharding import PartitionSpec as P
 
 FH = 1024
 EXPERTS = 16
+SPLIT = 4
+MOST = 3
 bf16, f32 = jnp.bfloat16, jnp.float32
 
 
@@ -105,6 +111,430 @@
     return mixed.transpose(1, 0, 2).reshape(own_rows, width)
 
 
+MIB = 1 << 20
+VM = pl.BlockSpec(memory_space=pltpu.VMEM)
+PAD = 128
+QUICK = pl.CostEstimate(flops=1, bytes_accessed=1, transcendentals=0)
+
+
+HB = pl.BlockSpec(memory_space=pltpu.HBM)
+
+
+def call(kernel, outs, *args, limit=4, scratch=(), far=0, inside=False):
+    return pl.pallas_call(
+        kernel,
+        in_specs=[VM] * (len(args) - far) + [HB] * far,
+        out_specs=[VM] * len(outs),
+        out_shape=[pltpu.VMEM(*o) for o in outs] if inside else [jax.ShapeDtypeStruct(*o) for o in outs],
+        scratch_shapes=list(scratch),
+        cost_estimate=QUICK,
+        compiler_params=pltpu.CompilerParams(vmem_limit_bytes=limit * MIB),
+    )(*args)
+
+
+def halves(v):
+    high = v.astype(bf16)
+    return high, (v - high.astype(f32)).astype(bf16)
+
+
+def column(table, i):
+    lane = lax.broadcasted_iota(jnp.int32, table.shape, 1)
+    return jnp.sum(jnp.where(lane == i, table, 0.0), 1, keepdims=True)
+
+
+def split_kernel(*refs):
+    inputs, outs, scratch, sem = refs[:6], refs[6:10], refs[10:16], refs[16]
+    heads, residual, routes, weights, gains, scales = scratch
+    send, keep, gain, scale = outs
+    copies = [
+        pltpu.make_async_copy(a.at[0] if i == 0 else a, t, sem.at[i])
+        for i, (a, t) in enumerate(zip(inputs, scratch))
+    ]
+    for copy in copies:
+        copy.start()
+    for copy in copies:
+        copy.wait()
+    c = lax.axis_index("cuts")
+    b = c & 1
+    rows, width = heads.shape
+    own = residual.shape[0]
+    n_c = rows // own
+    part = width // n_c
+    at = lax.broadcasted_iota(jnp.int32, (rows, 1), 0) // own == c
+
+    def wide(v):
+        return jnp.where(at, jnp.concatenate([v] * n_c, 0), 0.0)
+
+    for x in range(n_c // 2):
+        low = pl.ds(2 * x * part, part)
+        high = pl.ds((2 * x + 1) * part, part)
+        v0 = heads[:, low] + wide(residual[:, low].astype(f32))
+        v1 = heads[:, high] + wide(residual[:, high].astype(f32))
+        to = pl.ds(x * part, part)
+        keep[:, to] = jnp.where(b == 0, v0, v1)
+        send[:, to] = jnp.where(b == 0, v1, v0)
+    lane = lax.broadcasted_iota(jnp.int32, (own, PAD), 1)
+    share = jnp.zeros((own, PAD), f32)
+    for k in range(routes.shape[1]):
+        share = share + jnp.where(lane == routes[:, k : k + 1], weights[:, k : k + 1], 0.0)
+    share = wide(share)
+    end = pl.ds(n_c // 2 * part, PAD)
+    keep[:, end] = share
+    send[:, end] = share
+    scale[...] = scales[...]
+    lines = part // PAD
+    for i in range(lines):
+        gain[:, i * PAD : (i + 1) * PAD] = gains[pl.ds(c * lines + i, 1), :]
+
+
+def join_kernel(keep, got, send, left):
+    h = lax.axis_index("cuts") >> 1
+    part = left.shape[1] - PAD
+    v0 = keep[:, :part] + got[:, :part]
+    v1 = keep[:, part : 2 * part] + got[:, part : 2 * part]
+    share = keep[:, 2 * part :] + got[:, 2 * part :]
+    left[:, :part] = jnp.where(h == 0, v0, v1)
+    send[:, :part] = jnp.where(h == 0, v1, v0)
+    left[:, part:] = share
+    send[:, part:] = share
+
+
+def stream_kernel(left, got, gate, up, out, gate_out, up_out):
+    part = left.shape[1] - PAD
+    out[:, :part] = (left[:, :part] + got[:, :part]).astype(bf16)
+    high, low = halves(left[:, part:] + got[:, part:])
+    lane = lax.broadcasted_iota(jnp.int32, high.shape, 1)
+    low = pltpu.roll(jnp.where(lane < EXPERTS, low.astype(f32), 0.0), EXPERTS, 1)
+    out[:, part:] = (jnp.where(lane < EXPERTS, high.astype(f32), 0.0) + low).astype(bf16)
+
+
+def load_experts(experts, w_gate, w_up, outs, sem):
+    copies = []
+    for k, expert in enumerate(experts):
+        for w, out in ((w_gate, outs[2 * k]), (w_up, outs[2 * k + 1])):
+            at = pl.ds(pl.multiple_of(expert * FH, FH), FH)
+            n = len(copies)
+            step = w.shape[0] // SPLIT
+            for p in range(SPLIT):
+                rows = pl.ds(p * step, step)
+                copies.append(pltpu.make_async_copy(w.at[rows, at], out.at[rows], sem.at[n + p]))
+    for copy in copies:
+        copy.start()
+    return copies
+
+
+def expert_of(pair, other):
+    b = lax.axis_index("cuts") & 1
+    return 2 * pair + (1 - b if other else b)
+
+
+def loads(which, part, after, w_gate, w_up, limit, held=()):
+    n, h = 2 * len(which), len(held)
+
+    def kernel(*refs):
+        sem = refs[-1]
+        copies = load_experts(
+            [expert_of(*w) for w in which], refs[h + 1], refs[h + 2], refs[2 * h + 3 : -1], sem
+        )
+        for copy in copies:
+            copy.wait()
+
+    return pl.pallas_call(
+        kernel,
+        in_specs=[VM] * h + [HB] * 3,
+        out_specs=[VM] * (h + n),
+        out_shape=[pltpu.VMEM((part, FH), bf16)] * (h + n),
+        input_output_aliases={i: i for i in range(h)},
+        scratch_shapes=[pltpu.SemaphoreType.DMA((SPLIT * n,))],
+        cost_estimate=QUICK,
+        compiler_params=pltpu.CompilerParams(vmem_limit_bytes=limit * MIB),
+    )(*held, after, w_gate, w_up)
+
+
+def load_down_kernel(after, w_down, *refs):
+    outs, token, sem = refs[:-2], refs[-2], refs[-1]
+    copies = []
+    for i, (pair, other) in enumerate(((0, False), (0, True), (1, False), (1, True))):
+        at = pl.ds(pl.multiple_of(expert_of(pair, other) * FH, FH), FH)
+        copies.append(pltpu.make_async_copy(w_down.at[at], outs[i], sem.at[i]))
+    for copy in copies:
+        copy.start()
+    for copy in copies:
+        copy.wait()
+    token[...] = jnp.zeros_like(token)
+
+
+def expert_product(x, w_gate, w_up, out):
+    tile = 256
+    for w, base in ((w_gate, 0), (w_up, FH)):
+        for i in range(FH // tile):
+            p = jnp.dot(x[...], w[:, i * tile : (i + 1) * tile], preferred_element_type=f32)
+            out[:, pl.ds(base + i * tile, tile)] = p.astype(out.dtype)
+
+
+def first_kernel(s0, s1, s2, s3, gain, w_gate, w_up, x, send, share, square):
+    part = x.shape[1]
+    rows_e = s0.shape[0]
+    weight = gain[...]
+    for k, s in enumerate((s0, s1, s2, s3)):
+        v = s[:, :part].astype(f32)
+        at = pl.ds(k * rows_e, rows_e)
+        x[at, :] = (v * weight).astype(bf16)
+        square[at, :] = jnp.broadcast_to(jnp.sum(v * v, 1, keepdims=True), (rows_e, PAD))
+        t = s[:, part:].astype(f32)
+        lane = lax.broadcasted_iota(jnp.int32, t.shape, 1)
+        t = t + pltpu.roll(t, PAD - EXPERTS, 1)
+        share[at, :] = jnp.where(lane < EXPERTS, t, 0.0)
+    expert_product(x, w_gate, w_up, send)
+    send[:, 2 * FH :] = parts(square[...])
+
+
+def parts(v):
+    high, low = halves(v)
+    lane = lax.broadcasted_iota(jnp.int32, v.shape, 1)
+    return jnp.where(lane == 0, high.astype(f32), low.astype(f32)).astype(bf16)
+
+
+def pair_sum(t):
+    lane = lax.broadcasted_iota(jnp.int32, t.shape, 1)
+    return jnp.broadcast_to(jnp.sum(jnp.where(lane < 2, t, 0.0), 1, keepdims=True), t.shape)
+
+
+def product_kernel(x, w_gate, w_up, out):
+    expert_product(x, w_gate, w_up, out)
+
+
+def product_stream_kernel(x, gate_hbm, up_hbm, out, gate, up, sem):
+    expert = expert_of(1, False)
+    at = pl.ds(pl.multiple_of(expert * FH, FH), FH)
+    step = 256
+    parts_of = x.shape[1] // step
+    copies = []
+    for p in range(parts_of):
+        rows = pl.ds(p * step, step)
+        for w, t in ((gate_hbm, gate), (up_hbm, up)):
+            copies.append(pltpu.make_async_copy(w.at[rows, at], t.at[rows], sem.at[len(copies)]))
+    for copy in copies:
+        copy.start()
+    for p in range(parts_of):
+        rows = pl.ds(p * step, step)
+        for k, t in enumerate((gate, up)):
+            copies[2 * p + k].wait()
+            v = jnp.dot(x[:, rows], t[rows, :], preferred_element_type=f32)
+            to = pl.ds(k * FH, FH)
+            out[:, to] = v if p == 0 else out[:, to] + v
+
+
+def own_expert(pair):
+    e = lax.axis_index("expert")
+    return e * (EXPERTS // lax.axis_size("expert")) + expert_of(pair, False)
+
+
+def places(share, own_rows, slots):
+    rows = share.shape[0]
+    on = jnp.where(share != 0.0, 1.0, 0.0)
+    row = lax.broadcasted_iota(jnp.int32, (rows, 1), 0)
+    within = row % own_rows
+    before = jnp.zeros_like(on)
+    wide = jnp.broadcast_to(on, (rows, PAD))
+    for d in range(1, own_rows):
+        before = before + jnp.where(within >= d, pltpu.roll(wide, d, 0)[:, :1], 0.0)
+    slot = row // own_rows * MOST + before.astype(jnp.int32)
+    at = lax.broadcasted_iota(jnp.int32, (rows, slots), 1)
+    return jnp.where((at == slot) & (on != 0.0), 1.0, 0.0).astype(bf16)
+
+
+def packed(v, where):
+    dims = (((0,), (0,)), ((), ()))
+    return lax.dot_general(where, v, dims, preferred_element_type=f32).astype(bf16)
+
+
+def payload(v, square, share, pair, own_rows, send, place):
+    where = places(column(share[...], own_expert(pair)), own_rows, send.shape[0])
+    place[...] = where
+    send[:, : 2 * FH] = packed(v.astype(bf16), where)
+    send[:, 2 * FH :] = packed(parts(square), where)
+
+
+def first_sum_kernel(own_rows, keep, got, square, share, total, send, square_out, place):
+    v = keep[...] + got[:, : 2 * FH].astype(f32)
+    total[...] = v
+    s = square[...] + pair_sum(got[:, 2 * FH :].astype(f32))
+    square_out[...] = s
+    payload(v, s, share, 0, own_rows, send, place)
+
+
+def sum_kernel(own_rows, keep, got, square, share, total, send, place):
+    v = keep[...] + got[...].astype(f32)
+    total[...] = v
+    payload(v, square[...], share, 1, own_rows, send, place)
+
+
+def hidden_kernel(pair, width, total, got, square, place, share, scale, after, out):
+    squares = pair_sum(jnp.dot(place[...], got[:, 2 * FH :], preferred_element_type=f32))
+    factor = lax.rsqrt((square[...] + squares) / width + 1e-06)[:, :1]
+    expert = own_expert(pair)
+    coefficient = column(share[...], expert) * column(scale[...], expert)
+    v = jnp.dot(place[...], got[:, : 2 * FH], preferred_element_type=f32)
+    v = (total[...] + v) * factor
+    g, u = v[:, :FH], v[:, FH:]
+    out[...] = (g / (1.0 + jnp.exp(-g)) * u * coefficient).astype(bf16)
+
+
+def down_kernel(last, *refs):
+    if last:
+        hidden, w_down, before, o0, o1, o2, o3 = refs
+    elif len(refs) == 4:
+        hidden, w_down, before, out = refs
+    else:
+        (hidden, w_down, out), before = refs, None
+    tile = 256
+    for i in range(w_down.shape[1] // tile):
+        cols = pl.ds(i * tile, tile)
+        p = jnp.dot(hidden[...], w_down[:, cols], preferred_element_type=f32)
+        if before is not None:
+            p = p + before[:, cols]
+        if last:
+            r = o0.shape[0]
+            for k, o in enumerate((o0, o1, o2, o3)):
+                o[:, cols] = p[k * r : (k + 1) * r].astype(o.dtype)
+        else:
+            out[:, cols] = p
+
+
+def mixed_kernel(stream, own, r1, r2, r3, m0, m1, m2, m3):
+    c = lax.axis_index("cuts")
+    part = own.shape[1]
+    v = stream[:, :part].astype(f32) + own[...]
+    for r in (r1, r2, r3):
+        v = v + r[...].astype(f32)
+    n = m0.shape[0]
+    blocks = [v[k * n : (k + 1) * n] for k in range(4)]
+    for k, m in enumerate((m0, m1, m2, m3)):
+        to = c ^ k
+        t = jnp.where(to < 2, jnp.where(to == 0, blocks[0], blocks[1]),
+                      jnp.where(to == 2, blocks[2], blocks[3]))
+        m[...] = t.astype(bf16)
+
+
+def final_kernel(m0, m1, m2, m3, out):
+    c = lax.axis_index("cuts")
+    part = m0.shape[1]
+    p = [m[...].astype(f32) for m in (m0, m1, m2, m3)]
+    for s in range(4):
+        k = c ^ s
+        t = jnp.where(k < 2, jnp.where(k == 0, p[0], p[1]), jnp.where(k == 2, p[2], p[3]))
+        out[:, s * part : (s + 1) * part] = t.astype(bf16)
+
+
+def fast_body(
+    residual, head_partials, norm_gain, routes, route_weights, w_gate, w_up, w_down, expert_scale
+):
+    own_rows, width = residual.shape
+    rows_e = 4 * own_rows
+    part = width // 4
+    rows = 4 * rows_e
+    slots = rows // own_rows * MOST
+    weight = pltpu.VMEM((part, FH), bf16)
+
+    cut = (rows_e, 2 * part + PAD)
+    gains, scales = norm_gain.reshape(width // PAD, PAD), expert_scale.reshape(1, EXPERTS)
+    send, keep, gain, scale = call(
+        split_kernel, [(cut, f32)] * 2 + [((1, part), f32), ((1, EXPERTS), f32)],
+        head_partials, residual, routes, route_weights, gains, scales,
+        far=6, limit=62, inside=True,
+        scratch=[
+            pltpu.VMEM((rows_e, width), f32), pltpu.VMEM(residual.shape, bf16),
+            pltpu.VMEM(routes.shape, jnp.int32), pltpu.VMEM(route_weights.shape, f32),
+            pltpu.VMEM(gains.shape, f32), pltpu.VMEM(scales.shape, f32),
+            pltpu.SemaphoreType.DMA((6,)),
+        ],
+    )
+    cut = (rows_e, part + PAD)
+    send, left = call(join_kernel, [(cut, f32)] * 2, keep, swap(send, "cuts", 1))
+    got = swap(send, "cuts", 2)
+    ga0, ua0 = loads([(0, True)], part, send, w_gate, w_up, 42)
+    s0, ga0, ua0 = pl.pallas_call(
+        stream_kernel,
+        in_specs=[VM] * 4,
+        out_specs=[VM] * 3,
+        out_shape=[jax.ShapeDtypeStruct(cut, bf16), weight, weight],
+        input_output_aliases={2: 1, 3: 2},
+        cost_estimate=QUICK,
+        compiler_params=pltpu.CompilerParams(vmem_limit_bytes=4 * MIB),
+    )(left, got, ga0, ua0)
+    s3, s2, s1 = [swap(s0, "expert", k) for k in (3, 2, 1)]
+    ga0, ua0, gb0, ub0, ga1, ua1 = loads(
+        [(0, False), (1, True)], part, s0, w_gate, w_up, 29, (ga0, ua0)
+    )
+
+    x, send, share, square = call(
+        first_kernel,
+        [((rows, part), bf16), ((rows, 2 * FH + PAD), bf16), ((rows, PAD), f32), ((rows, PAD), f32)],
+        s0, s1, s2, s3, gain, ga0, ua0,
+    )
+    got = swap(send, "cuts", 1)
+    full = ((rows, 2 * FH), f32)
+    (keep,) = call(product_kernel, [full], x, gb0, ub0)
+    table = ((rows, PAD), f32)
+    sent_all = ((rows, 2 * FH), bf16)
+    place = ((rows, slots), bf16)
+    sent = ((slots, 2 * FH + PAD), bf16)
+    total0, send, square, place0 = call(
+        functools.partial(first_sum_kernel, own_rows),
+        [full, sent, table, place], keep, got, square, share,
+    )
+    got0 = swap(send, "cuts", 2)
+    (send,) = call(product_kernel, [sent_all], x, ga1, ua1)
+    got = swap(send, "cuts", 1)
+    (keep,) = call(
+        product_stream_kernel, [full], x, w_gate, w_up, far=2, limit=40,
+        scratch=[
+            pltpu.VMEM((part, FH), bf16), pltpu.VMEM((part, FH), bf16),
+            pltpu.SemaphoreType.DMA((2 * (part // 256),)),
+        ],
+    )
+    total1, send, place1 = call(
+        functools.partial(sum_kernel, own_rows), [full, sent, place], keep, got, square, share
+    )
+    got1 = swap(send, "cuts", 2)
+    d0, d1, d2, d3, after = pl.pallas_call(
+        load_down_kernel,
+        in_specs=[HB] * 2,
+        out_specs=[VM] * 5,
+        out_shape=[pltpu.VMEM((FH, part), bf16)] * 4 + [jax.ShapeDtypeStruct((8, PAD), f32)],
+        scratch_shapes=[pltpu.SemaphoreType.DMA((4,))],
+        cost_estimate=QUICK,
+        compiler_params=pltpu.CompilerParams(vmem_limit_bytes=34 * MIB),
+    )(send, w_down)
+
+    half = ((rows, FH), bf16)
+    out = ((rows, part), f32)
+    (h0,) = call(
+        functools.partial(hidden_kernel, 0, width), [half],
+        total0, got0, square, place0, share, scale, after,
+    )
+    g0 = swap(h0, "cuts", 1)
+    (t,) = call(functools.partial(down_kernel, False), [out], h0, d0)
+    (t,) = call(functools.partial(down_kernel, False), [out], g0, d1, t)
+    (h1,) = call(
+        functools.partial(hidden_kernel, 1, width), [half],
+        total1, got1, square, place1, share, scale, after,
+    )
+    g1 = swap(h1, "cuts", 1)
+    (t,) = call(functools.partial(down_kernel, False), [out], h1, d2, t)
+    o0, o1, o2, o3 = call(
+        functools.partial(down_kernel, True),
+        [((rows_e, part), f32)] + [((rows_e, part), bf16)] * 3,
+        g1, d3, t,
+    )
+    r3, r2, r1 = [swap(o, "expert", k) for k, o in ((3, o3), (2, o2), (1, o1))]
+    m0, m1, m2, m3 = call(mixed_kernel, [((own_rows, part), bf16)] * 4, s0, o0, r1, r2, r3)
+    m2, m3, m1 = [swap(m, "cuts", k) for k, m in ((2, m2), (3, m3), (1, m1))]
+    (mixed,) = call(final_kernel, [((own_rows, width), bf16)], m0, m1, m2, m3)
+    return mixed
+
+
 def solution(mesh):
     in_specs = (
         P(("group", "expert", "cuts"), None),
@@ -118,4 +548,7 @@
         P(),
     )
     out_specs = P(("group", "expert", "cuts"), None)
-    return jax.shard_map(body, mesh=mesh, in_specs=in_specs, out_specs=out_specs, check_vma=False)
+    small = mesh.shape["expert"] == 4 and mesh.shape["cuts"] == 4
+    return jax.shard_map(
+        fast_body if small else body, mesh=mesh, in_specs=in_specs, out_specs=out_specs, check_vma=False
+    )

time: 94.2 us -> 56.6 us (0.60)
  Pallas kernels: 0 us -> 28.2 us
  blocking collectives: 25.2 us -> 0 us
  matrix products: 23.7 us -> 0 us
  waiting for transfers between devices: 20.9 us -> 10.9 us
  local copies, waits for them, and re-layouts: 6.16 us -> 0 us
  other arithmetic: 2.03 us -> 0 us
  starting transfers between devices: 15.6 us -> 17.2 us
    pallas_call x0 -> x20, Pallas kernels: none -> 28.2 us  [the longest x16 14.3 us: call(): pl.pallas_call(kernel, in_specs=[VM] * (len(args) - far) + [HB] * far, ou...]
    dot_general x4 -> x0, matrix products: 23.7 us -> none  [the longest x2 15.7 us: product(): p = jnp.dot(x, w, preferred_element_type=f32).astype(bf16)]
    all_gather x1 -> x0, blocking collectives: 18.7 us -> none  [body(): share = lax.all_gather(share, ('expert', 'cuts'), axis=0, tiled=True)]
    ppermute x8 -> x17, starting transfers between devices: 6.76 us -> 17.2 us  [swap(): return lax.ppermute(x, axis, [(i, i ^ bit) for i in range(n)])]
    ppermute x6 -> x0, waiting for transfers between devices: 9.58 us -> none  [shift(): return lax.ppermute(x, axis, [(i, (i + k) % n) for i in range(n)])]
    ppermute x6 -> x0, starting transfers between devices: 8.79 us -> none  [shift(): return lax.ppermute(x, axis, [(i, (i + k) % n) for i in range(n)])]
    all_to_all x1 -> x0, blocking collectives: 6.44 us -> none  [body(): lax.all_to_all(mixed.reshape(n_c, own_rows, part), 'cuts', split_axis=0,...]
    unnamed x9 -> x0, local copies, waits for them, and re-layouts: 1.68 us -> none
  transfers between devices with their start and end apart: 14 -> 17, of which waited for: 10 -> 8; matrix products, arithmetic and copies ran while one was open for 2% -> 0% of each run, Pallas kernels for 0% -> 42%
where the time goes in v2:
time: 56.6 us; the launch traced here: 56.5 us
  Pallas kernels  28.2 us (50%)
  starting transfers between devices  17.2 us (30%)
  waiting for transfers between devices  10.9 us (19%)
    ppermute x17, starting transfers between devices, swap(): return lax.ppermute(x, axis, [(i, i ^ bit) for i in range(n)])  17.2 us
    pallas_call x16, Pallas kernels, call(): pl.pallas_call(kernel, in_specs=[VM] * (len(args) - far) + [HB] * far, ou...  14.3 us
    ppermute x17, waiting for transfers between devices, swap(): return lax.ppermute(x, axis, [(i, i ^ bit) for i in range(n)])  10.9 us
    pallas_call x2, Pallas kernels, loads(): pl.pallas_call(kernel, in_specs=[VM] * h + [HB] * 3, out_specs=[VM] * (h...  8.57 us
    pallas_call x1, Pallas kernels, fast_body(): pl.pallas_call(load_down_kernel, in_specs=[HB] * 2, out_specs=[VM] * 5, o...  5.28 us
  transfers between devices with their start and end apart: 17, of which 8 were waited for; matrix products, arithmetic and copies ran while one was open for 0% of the time, Pallas kernels for 42%

profile of v2, /device:TPU:0, one launch (start us, length us, event | category | flops | bytes accessed | tf_op | source)
XLA Modules:
  0.0 56.5 jit_solution(2784659669971640879)
XLA Ops:
  0.0 1.2 %shard_map.91 = (f32[16,3712]{1,0:T(8,128)S(1)}, f32[16,3712]{1,0:T(8,128)S(1)}, f32[1,1792]{1,0:T(1,128)S(1)}, f32[1,16]{1,0:T(1,128)S(1)}) custom-call(f32[1,16,7168]{2,1,0:T(8,128)} %refs_0_.1, bf16[4,7168]{1,0:T(4,128)(2,1)} %refs_1_.2, s32[4,8]{1,0:T(4,128)} %refs_2_.2, f32[4,8]{1,0:T(4,128)} %refs_3_.2, f32[56,128]{1,0:T(8,128)} %bitcast.2, ...), custom_call_target="tpu_custom_call" | custom-call | flops 1 | bytes 1 | tf_op jit(solution)/shard_map/pallas_call | solution.py:124
  1.7 1.1 %collective-permute-done.got = f32[16,3712]{1,0:T(8,128)S(1)} collective-permute-done((f32[16,3712]{1,0:T(8,128)S(1)}, f32[16,3712]{1,0:T(8,128)S(1)}, u32[]{:S(2)}, u32[]{:S(2)}) %collective-permute-start) | collective-permute-done | bytes 237600 | tf_op jit(solution)/shard_map/ppermute | solution.py:24
  2.9 2.9 %collective-permute-start.1 = (f32[16,1920]{1,0:T(8,128)S(1)}, f32[16,1920]{1,0:T(8,128)S(1)}, u32[]{:S(2)}, u32[]{:S(2)}) collective-permute-start(f32[16,1920]{1,0:T(8,128)S(1)} %get-tuple-element.49.refs_0_), channel_id=1, source_target_pairs={{0,2},{1,3},{2,0},{3,1},{4,6},{5,7},{6,4},{7,5},{8,10},{9,11},{10,... | collective-permute-start | bytes 368648 | tf_op jit(solution)/shard_map/ppermute | solution.py:24
  5.8 3.2 %shard_map.93 = (bf16[1792,1024]{1,0:T(8,128)(2,1)S(1)}, bf16[1792,1024]{1,0:T(8,128)(2,1)S(1)}) custom-call(f32[16,1920]{1,0:T(8,128)S(1)} %get-tuple-element.49.refs_0_, bf16[1792,4096]{1,0:T(8,128)(2,1)} %gate_hbm.1, bf16[1792,4096]{1,0:T(8,128)(2,1)} %up_hbm.1), custom_call_target="tpu_custom_call" | custom-call | flops 1 | bytes 1 | tf_op jit(solution)/shard_map/pallas_call | solution.py:242
  9.5 1.8 %collective-permute-start.2 = (bf16[16,1920]{1,0:T(8,128)(2,1)S(1)}, bf16[16,1920]{1,0:T(8,128)(2,1)S(1)}, u32[]{:S(2)}, u32[]{:S(2)}) collective-permute-start(bf16[16,1920]{1,0:T(8,128)(2,1)S(1)} %get-tuple-element.52.refs_2_.s0.stream), channel_id=1, source_target_pairs={{0,4},{4,0},{8,12},{12,8},{1,5},{5,1},{9,13},{13,9},{2,6},{6,2},{1... | collective-permute-start | bytes 184328 | tf_op jit(solution)/shard_map/ppermute | solution.py:24
  11.3 2.6 %collective-permute-start.3 = (bf16[16,1920]{1,0:T(8,128)(2,1)S(1)}, bf16[16,1920]{1,0:T(8,128)(2,1)S(1)}, u32[]{:S(2)}, u32[]{:S(2)}) collective-permute-start(bf16[16,1920]{1,0:T(8,128)(2,1)S(1)} %get-tuple-element.52.refs_2_.s0.stream), channel_id=1, source_target_pairs={{0,8},{4,12},{8,0},{12,4},{1,9},{5,13},{9,1},{13,5},{2,10},{6,14},... | collective-permute-start | bytes 184328 | tf_op jit(solution)/shard_map/ppermute | solution.py:24
  13.9 5.4 %shard_map.95 = (bf16[1792,1024]{1,0:T(8,128)(2,1)S(1)}, bf16[1792,1024]{1,0:T(8,128)(2,1)S(1)}, bf16[1792,1024]{1,0:T(8,128)(2,1)S(1)}, bf16[1792,1024]{1,0:T(8...) custom-call(bf16[1792,1024]{1,0:T(8,128)(2,1)S(1)} %get-tuple-elemen, ...), custom_call_target="tpu_custom_call", output_to_operand_aliasing={{0}: (0, {}), {1}: (1, {})} | custom-call | flops 1 | bytes 1 | tf_op jit(solution)/shard_map/pallas_call | solution.py:242
  19.9 1.4 %shard_map.96 = (bf16[64,1792]{1,0:T(8,128)(2,1)S(1)}, bf16[64,2176]{1,0:T(8,128)(2,1)S(1)}, f32[64,128]{1,0:T(8,128)S(1)}, f32[64,128]{1,0:T(8,128)S(1)}) custom-call(bf16[16,1920]{1,0:T(8,128)(2,1)S(1)} %get-tuple-element.52.refs_2_.s0.stream, bf16[16,1920]{1,0:T(8,128)(2,1)S(1)} %collective-permute-done.2.s1, ...), custom_call_target="tpu_custom_call" | custom-call | flops 1 | bytes 1 | tf_op jit(solution)/shard_map/pallas_call | solution.py:124
  21.4 1.4 %shard_map.98 = bf16[64,2048]{1,0:T(8,128)(2,1)S(1)} custom-call(bf16[64,1792]{1,0:T(8,128)(2,1)S(1)} %get-tuple-element.58.x, bf16[1792,1024]{1,0:T(8,128)(2,1)S(1)} %get-tuple-element.59.w_gate, bf16[1792,1024]{1,0:T(8,128)(2,1)S(1)} %get-tuple-element.60.w_up), custom_call_target="tpu_custom_call" | custom-call | flops 1 | bytes 1 | tf_op jit(solution)/shard_map/pallas_call | solution.py:124
  23.4 1.4 %shard_map.99.keep = f32[64,2048]{1,0:T(8,128)S(1)} custom-call(bf16[64,1792]{1,0:T(8,128)(2,1)S(1)} %get-tuple-element.58.x, bf16[1792,1024]{1,0:T(8,128)(2,1)S(1)} %get-tuple-element.61.w_gate, bf16[1792,1024]{1,0:T(8,128)(2,1)S(1)} %get-tuple-element.62.w_up), custom_call_target="tpu_custom_call" | custom-call | flops 1 | bytes 1 | tf_op jit(solution)/shard_map/pallas_call | solution.py:124
  25.2 1.6 %collective-permute-start.9 = (bf16[48,2176]{1,0:T(8,128)(2,1)S(1)}, bf16[48,2176]{1,0:T(8,128)(2,1)S(1)}, u32[]{:S(2)}, u32[]{:S(2)}) collective-permute-start(bf16[48,2176]{1,0:T(8,128)(2,1)S(1)} %get-tuple-element.75), channel_id=1, source_target_pairs={{0,2},{1,3},{2,0},{3,1},{4,6},{5,7},{6,4},{7,5},{8,10},{9,11},{10,... | collective-permute-start | bytes 626696 | tf_op jit(solution)/shard_map/ppermute | solution.py:24
  26.8 3.5 %shard_map.97.keep = f32[64,2048]{1,0:T(8,128)S(1)} custom-call(bf16[64,1792]{1,0:T(8,128)(2,1)S(1)} %get-tuple-element.58.x, bf16[1792,4096]{1,0:T(8,128)(2,1)} %gate_hbm.1, bf16[1792,4096]{1,0:T(8,128)(2,1)} %up_hbm.1), custom_call_target="tpu_custom_call" | custom-call | flops 1 | bytes 1 | tf_op jit(solution)/shard_map/pallas_call | solution.py:124
  31.3 5.3 %shard_map.102 = (bf16[1024,1792]{1,0:T(8,128)(2,1)S(1)}, bf16[1024,1792]{1,0:T(8,128)(2,1)S(1)}, bf16[1024,1792]{1,0:T(8,128)(2,1)S(1)}, bf16[1024,1792]{1,0:T(8,128)(2,1)S(1)}, f32[8,128]{1,0:T(8,128)S(1)}) custom-call(bf16[48,2176]{1,0:T(8,128)(2,1)S(1)} %get-tuple-element.68.after, bf16[4096,1792]{1,0:T(8,128)(2,1)} %w_down.1), custom_call_target="tpu_custom_call" | custom-call | flops 1 | bytes 1 | tf_op jit(solution)/shard_map/pallas_call | solution.py:501
  38.0 0.8 %shard_map.105.refs_2_ = f32[64,1792]{1,0:T(8,128)S(1)} custom-call(bf16[64,1024]{1,0:T(8,128)(2,1)S(1)} %shard_map.104.refs_0_, bf16[1024,1792]{1,0:T(8,128)(2,1)S(1)} %get-tuple-element.78.refs_1_), custom_call_target="tpu_custom_call" | custom-call | flops 1 | bytes 1 | tf_op jit(solution)/shard_map/pallas_call | solution.py:124
  38.8 0.8 %shard_map.106.refs_2_ = f32[64,1792]{1,0:T(8,128)S(1)} custom-call(bf16[64,1024]{1,0:T(8,128)(2,1)S(1)} %collective-permute-done.10.refs_0_, bf16[1024,1792]{1,0:T(8,128)(2,1)S(1)} %get-tuple-element.77.refs_1_, f32[64,1792]{1,0:T(8,128)S(1)} %shard_map.105.refs_2_), custom_call_target="tpu_custom_call" | custom-call | flops 1 | bytes 1 | tf_op jit(solution)/shard_map/pallas_call | solution.py:124
  39.6 0.8 %shard_map.107.refs_2_ = f32[64,1792]{1,0:T(8,128)S(1)} custom-call(bf16[64,1024]{1,0:T(8,128)(2,1)S(1)} %shard_map.103.refs_0_, bf16[1024,1792]{1,0:T(8,128)(2,1)S(1)} %get-tuple-element.73.refs_1_, f32[64,1792]{1,0:T(8,128)S(1)} %shard_map.106.refs_2_), custom_call_target="tpu_custom_call" | custom-call | flops 1 | bytes 1 | tf_op jit(solution)/shard_map/pallas_call | solution.py:124
  40.4 0.8 %shard_map.108 = (f32[16,1792]{1,0:T(8,128)S(1)}, bf16[16,1792]{1,0:T(8,128)(2,1)S(1)}, bf16[16,1792]{1,0:T(8,128)(2,1)S(1)}, bf16[16,1792]{1,0:T(8,128)(2,1)S(1)}) custom-call(bf16[64,1024]{1,0:T(8,128)(2,1)S(1)} %collective-permute-done.8.refs_0_, bf16[1024,1792]{1,0:T(8,128)(2,1)S(1)} %get-tuple-element.72.refs_1_, f32[64,1792]{1,0:T(8,128)S(1)} %shard_map.107.refs_2_), custom_call_target="tpu_custom_call" | custom-call | flops 1 | bytes 1 | tf_op jit(solution)/shard_map/pallas_call | solution.py:124
  41.5 3.5 %collective-permute-start.12 = (bf16[16,1792]{1,0:T(8,128)(2,1)S(1)}, bf16[16,1792]{1,0:T(8,128)(2,1)S(1)}, u32[]{:S(2)}, u32[]{:S(2)}) collective-permute-start(bf16[16,1792]{1,0:T(8,128)(2,1)S(1)} %get-tuple-element.81), channel_id=1, source_target_pairs={{0,8},{4,12},{8,0},{12,4},{1,9},{5,13},{9,1},{13,5},{2,10},{6,14},... | collective-permute-start | bytes 172040 | tf_op jit(solution)/shard_map/ppermute | solution.py:24
  45.6 3.1 %collective-permute-done.12.r2 = bf16[16,1792]{1,0:T(8,128)(2,1)S(1)} collective-permute-done((bf16[16,1792]{1,0:T(8,128)(2,1)S(1)}, bf16[16,1792]{1,0:T(8,128)(2,1)S(1)}, u32[]{:S(2)}, u32[]{:S(2)}) %collective-permute-start.12) | collective-permute-done | bytes 57376 | tf_op jit(solution)/shard_map/ppermute | solution.py:24
  48.8 2.2 %collective-permute-done.13.r3 = bf16[16,1792]{1,0:T(8,128)(2,1)S(1)} collective-permute-done((bf16[16,1792]{1,0:T(8,128)(2,1)S(1)}, bf16[16,1792]{1,0:T(8,128)(2,1)S(1)}, u32[]{:S(2)}, u32[]{:S(2)}) %collective-permute-start.13) | collective-permute-done | bytes 57376 | tf_op jit(solution)/shard_map/ppermute | solution.py:24
  51.2 1.5 %collective-permute-start.15 = (bf16[4,1792]{1,0:T(4,128)(2,1)S(1)}, bf16[4,1792]{1,0:T(4,128)(2,1)S(1)}, u32[]{:S(2)}, u32[]{:S(2)}) collective-permute-start(bf16[4,1792]{1,0:T(4,128)(2,1)S(1)} %get-tuple-element.85), channel_id=1, source_target_pairs={{0,2},{1,3},{2,0},{3,1},{4,6},{5,7},{6,4},{7,5},{8,10},{9,11},{10,... | collective-permute-start | bytes 43016 | tf_op jit(solution)/shard_map/ppermute | solution.py:24
  53.0 1.9 %collective-permute-done.15.m2 = bf16[4,1792]{1,0:T(4,128)(2,1)S(1)} collective-permute-done((bf16[4,1792]{1,0:T(4,128)(2,1)S(1)}, bf16[4,1792]{1,0:T(4,128)(2,1)S(1)}, u32[]{:S(2)}, u32[]{:S(2)}) %collective-permute-start.15) | collective-permute-done | bytes 14368 | tf_op jit(solution)/shard_map/ppermute | solution.py:24
  54.9 0.9 %collective-permute-done.16.m3 = bf16[4,1792]{1,0:T(4,128)(2,1)S(1)} collective-permute-done((bf16[4,1792]{1,0:T(4,128)(2,1)S(1)}, bf16[4,1792]{1,0:T(4,128)(2,1)S(1)}, u32[]{:S(2)}, u32[]{:S(2)}) %collective-permute-start.16) | collective-permute-done | bytes 14368 | tf_op jit(solution)/shard_map/ppermute | solution.py:24
  55.8 0.7 %shard_map.110 = bf16[4,7168]{1,0:T(4,128)(2,1)} custom-call(bf16[4,1792]{1,0:T(4,128)(2,1)S(1)} %get-tuple-element.83.m0, bf16[4,1792]{1,0:T(4,128)(2,1)S(1)} %collective-permute-done.14.m1, bf16[4,1792]{1,0:T(4,128)(2,1)S(1)} %collective-permute-done.15.m2, bf16[4,1792]{1,0:T(4,128)(2,1)S(1)} %collective-permute-done.16.m3), custom_call_target="tpu_custom_call" | custom-call | flops 1 | bytes 1 | tf_op jit(solution)/shard_map/pallas_call | solution.py:124
  (30 shorter events, 6.6 us)
Async XLA Ops:
  1.2 1.6 %collective-permute-start = (f32[16,3712]{1,0:T(8,128)S(1)}, f32[16,3712]{1,0:T(8,128)S(1)}, u32[]{:S(2)}, u32[]{:S(2)}) collective-permute-start(f32[16,3712]{1,0:T(8,128)S(1)} %get-tuple-element.47), channel_id=1, source_target_pairs={{0,1},{1,0},{2,3},{3,2},{4,5},{5,4},{6,7},{7,6},{8,9},{9,8},{10,11... | collective-permute-start | bytes 712712 | tf_op jit(solution)/shard_map/ppermute | solution.py:24
  2.9 6.5 %collective-permute-start.1 = (f32[16,1920]{1,0:T(8,128)S(1)}, f32[16,1920]{1,0:T(8,128)S(1)}, u32[]{:S(2)}, u32[]{:S(2)}) collective-permute-start(f32[16,1920]{1,0:T(8,128)S(1)} %get-tuple-element.49.refs_0_), channel_id=1, source_target_pairs={{0,2},{1,3},{2,0},{3,1},{4,6},{5,7},{6,4},{7,5},{8,10},{9,11},{10,... | collective-permute-start | bytes 368648 | tf_op jit(solution)/shard_map/ppermute | solution.py:24
  9.5 9.8 %collective-permute-start.2 = (bf16[16,1920]{1,0:T(8,128)(2,1)S(1)}, bf16[16,1920]{1,0:T(8,128)(2,1)S(1)}, u32[]{:S(2)}, u32[]{:S(2)}) collective-permute-start(bf16[16,1920]{1,0:T(8,128)(2,1)S(1)} %get-tuple-element.52.refs_2_.s0.stream), channel_id=1, source_target_pairs={{0,4},{4,0},{8,12},{12,8},{1,5},{5,1},{9,13},{13,9},{2,6},{6,2},{1... | collective-permute-start | bytes 184328 | tf_op jit(solution)/shard_map/ppermute | solution.py:24
  11.3 8.0 %collective-permute-start.3 = (bf16[16,1920]{1,0:T(8,128)(2,1)S(1)}, bf16[16,1920]{1,0:T(8,128)(2,1)S(1)}, u32[]{:S(2)}, u32[]{:S(2)}) collective-permute-start(bf16[16,1920]{1,0:T(8,128)(2,1)S(1)} %get-tuple-element.52.refs_2_.s0.stream), channel_id=1, source_target_pairs={{0,8},{4,12},{8,0},{12,4},{1,9},{5,13},{9,1},{13,5},{2,10},{6,14},... | collective-permute-start | bytes 184328 | tf_op jit(solution)/shard_map/ppermute | solution.py:24
  13.9 6.0 %collective-permute-start.4 = (bf16[16,1920]{1,0:T(8,128)(2,1)S(1)}, bf16[16,1920]{1,0:T(8,128)(2,1)S(1)}, u32[]{:S(2)}, u32[]{:S(2)}) collective-permute-start(bf16[16,1920]{1,0:T(8,128)(2,1)S(1)} %get-tuple-element.52.refs_2_.s0.stream), channel_id=1, source_target_pairs={{0,12},{4,8},{8,4},{12,0},{1,13},{5,9},{9,5},{13,1},{2,14},{6,10},... | collective-permute-start | bytes 184328 | tf_op jit(solution)/shard_map/ppermute | solution.py:24
  21.3 3.4 %collective-permute-start.6 = (bf16[64,2176]{1,0:T(8,128)(2,1)S(1)}, bf16[64,2176]{1,0:T(8,128)(2,1)S(1)}, u32[]{:S(2)}, u32[]{:S(2)}) collective-permute-start(bf16[64,2176]{1,0:T(8,128)(2,1)S(1)} %get-tuple-element.63), channel_id=1, source_target_pairs={{0,1},{1,0},{2,3},{3,2},{4,5},{5,4},{6,7},{7,6},{8,9},{9,8},{10,11... | collective-permute-start | bytes 835592 | tf_op jit(solution)/shard_map/ppermute | solution.py:24
  22.8 7.4 %collective-permute-start.5 = (bf16[64,2048]{1,0:T(8,128)(2,1)S(1)}, bf16[64,2048]{1,0:T(8,128)(2,1)S(1)}, u32[]{:S(2)}, u32[]{:S(2)}) collective-permute-start(bf16[64,2048]{1,0:T(8,128)(2,1)S(1)} %shard_map.98), channel_id=1, source_target_pairs={{0,1},{1,0},{2,3},{3,2},{4,5},{5,4},{6,7},{7,6},{8,9},{9,8},{10,11... | collective-permute-start | bytes 786440 | tf_op jit(solution)/shard_map/ppermute | solution.py:24
  25.2 11.4 %collective-permute-start.9 = (bf16[48,2176]{1,0:T(8,128)(2,1)S(1)}, bf16[48,2176]{1,0:T(8,128)(2,1)S(1)}, u32[]{:S(2)}, u32[]{:S(2)}) collective-permute-start(bf16[48,2176]{1,0:T(8,128)(2,1)S(1)} %get-tuple-element.75), channel_id=1, source_target_pairs={{0,2},{1,3},{2,0},{3,1},{4,6},{5,7},{6,4},{7,5},{8,10},{9,11},{10,... | collective-permute-start | bytes 626696 | tf_op jit(solution)/shard_map/ppermute | solution.py:24
  30.7 6.9 %collective-permute-start.7 = (bf16[48,2176]{1,0:T(8,128)(2,1)S(1)}, bf16[48,2176]{1,0:T(8,128)(2,1)S(1)}, u32[]{:S(2)}, u32[]{:S(2)}) collective-permute-start(bf16[48,2176]{1,0:T(8,128)(2,1)S(1)} %get-tuple-element.68.after), channel_id=1, source_target_pairs={{0,2},{1,3},{2,0},{3,1},{4,6},{5,7},{6,4},{7,5},{8,10},{9,11},{10,... | collective-permute-start | bytes 626696 | tf_op jit(solution)/shard_map/ppermute | solution.py:24
  37.0 1.8 %collective-permute-start.10 = (bf16[64,1024]{1,0:T(8,128)(2,1)S(1)}, bf16[64,1024]{1,0:T(8,128)(2,1)S(1)}, u32[]{:S(2)}, u32[]{:S(2)}) collective-permute-start(bf16[64,1024]{1,0:T(8,128)(2,1)S(1)} %shard_map.104.refs_0_), channel_id=1, source_target_pairs={{0,1},{1,0},{2,3},{3,2},{4,5},{5,4},{6,7},{7,6},{8,9},{9,8},{10,11... | collective-permute-start | bytes 393224 | tf_op jit(solution)/shard_map/ppermute | solution.py:24
  38.0 2.4 %collective-permute-start.8 = (bf16[64,1024]{1,0:T(8,128)(2,1)S(1)}, bf16[64,1024]{1,0:T(8,128)(2,1)S(1)}, u32[]{:S(2)}, u32[]{:S(2)}) collective-permute-start(bf16[64,1024]{1,0:T(8,128)(2,1)S(1)} %shard_map.103.refs_0_), channel_id=1, source_target_pairs={{0,1},{1,0},{2,3},{3,2},{4,5},{5,4},{6,7},{7,6},{8,9},{9,8},{10,11... | collective-permute-start | bytes 393224 | tf_op jit(solution)/shard_map/ppermute | solution.py:24
  41.2 4.5 %collective-permute-start.11 = (bf16[16,1792]{1,0:T(8,128)(2,1)S(1)}, bf16[16,1792]{1,0:T(8,128)(2,1)S(1)}, u32[]{:S(2)}, u32[]{:S(2)}) collective-permute-start(bf16[16,1792]{1,0:T(8,128)(2,1)S(1)} %get-tuple-element.80), channel_id=1, source_target_pairs={{0,4},{4,0},{8,12},{12,8},{1,5},{5,1},{9,13},{13,9},{2,6},{6,2},{1... | collective-permute-start | bytes 172040 | tf_op jit(solution)/shard_map/ppermute | solution.py:24
  41.5 7.2 %collective-permute-start.12 = (bf16[16,1792]{1,0:T(8,128)(2,1)S(1)}, bf16[16,1792]{1,0:T(8,128)(2,1)S(1)}, u32[]{:S(2)}, u32[]{:S(2)}) collective-permute-start(bf16[16,1792]{1,0:T(8,128)(2,1)S(1)} %get-tuple-element.81), channel_id=1, source_target_pairs={{0,8},{4,12},{8,0},{12,4},{1,9},{5,13},{9,1},{13,5},{2,10},{6,14},... | collective-permute-start | bytes 172040 | tf_op jit(solution)/shard_map/ppermute | solution.py:24
  45.0 6.0 %collective-permute-start.13 = (bf16[16,1792]{1,0:T(8,128)(2,1)S(1)}, bf16[16,1792]{1,0:T(8,128)(2,1)S(1)}, u32[]{:S(2)}, u32[]{:S(2)}) collective-permute-start(bf16[16,1792]{1,0:T(8,128)(2,1)S(1)} %get-tuple-element.82), channel_id=1, source_target_pairs={{0,12},{4,8},{8,4},{12,0},{1,13},{5,9},{9,5},{13,1},{2,14},{6,10},... | collective-permute-start | bytes 172040 | tf_op jit(solution)/shard_map/ppermute | solution.py:24
  51.1 1.9 %collective-permute-start.14 = (bf16[4,1792]{1,0:T(4,128)(2,1)S(1)}, bf16[4,1792]{1,0:T(4,128)(2,1)S(1)}, u32[]{:S(2)}, u32[]{:S(2)}) collective-permute-start(bf16[4,1792]{1,0:T(4,128)(2,1)S(1)} %get-tuple-element.84), channel_id=1, source_target_pairs={{0,1},{1,0},{2,3},{3,2},{4,5},{5,4},{6,7},{7,6},{8,9},{9,8},{10,11... | collective-permute-start | bytes 43016 | tf_op jit(solution)/shard_map/ppermute | solution.py:24
  51.2 3.8 %collective-permute-start.15 = (bf16[4,1792]{1,0:T(4,128)(2,1)S(1)}, bf16[4,1792]{1,0:T(4,128)(2,1)S(1)}, u32[]{:S(2)}, u32[]{:S(2)}) collective-permute-start(bf16[4,1792]{1,0:T(4,128)(2,1)S(1)} %get-tuple-element.85), channel_id=1, source_target_pairs={{0,2},{1,3},{2,0},{3,1},{4,6},{5,7},{6,4},{7,5},{8,10},{9,11},{10,... | collective-permute-start | bytes 43016 | tf_op jit(solution)/shard_map/ppermute | solution.py:24
  52.7 3.1 %collective-permute-start.16 = (bf16[4,1792]{1,0:T(4,128)(2,1)S(1)}, bf16[4,1792]{1,0:T(4,128)(2,1)S(1)}, u32[]{:S(2)}, u32[]{:S(2)}) collective-permute-start(bf16[4,1792]{1,0:T(4,128)(2,1)S(1)} %get-tuple-element.86), channel_id=1, source_target_pairs={{0,3},{1,2},{2,1},{3,0},{4,7},{5,6},{6,5},{7,4},{8,11},{9,10},{10,... | collective-permute-start | bytes 43016 | tf_op jit(solution)/shard_map/ppermute | solution.py:24

commit v3 on v2

--- a/solution.py
+++ b/solution.py
@@ -114,20 +114,23 @@
 MIB = 1 << 20
 VM = pl.BlockSpec(memory_space=pltpu.VMEM)
 PAD = 128
-QUICK = pl.CostEstimate(flops=1, bytes_accessed=1, transcendentals=0)
+COVER = 1 << 33
 
 
 HB = pl.BlockSpec(memory_space=pltpu.HBM)
 
 
-def call(kernel, outs, *args, limit=4, scratch=(), far=0, inside=False):
+def call(kernel, outs, *args, limit=4, scratch=(), far=0, inside=False, cost=1):
     return pl.pallas_call(
         kernel,
         in_specs=[VM] * (len(args) - far) + [HB] * far,
         out_specs=[VM] * len(outs),
-        out_shape=[pltpu.VMEM(*o) for o in outs] if inside else [jax.ShapeDtypeStruct(*o) for o in outs],
+        out_shape=[
+            o if not isinstance(o, tuple) else pltpu.VMEM(*o) if inside else jax.ShapeDtypeStruct(*o)
+            for o in outs
+        ],
         scratch_shapes=list(scratch),
-        cost_estimate=QUICK,
+        cost_estimate=pl.CostEstimate(flops=cost, bytes_accessed=1, transcendentals=0),
         compiler_params=pltpu.CompilerParams(vmem_limit_bytes=limit * MIB),
     )(*args)
 
@@ -187,6 +190,19 @@
         gain[:, i * PAD : (i + 1) * PAD] = gains[pl.ds(c * lines + i, 1), :]
 
 
+def share_parts(v):
+    high, low = halves(v)
+    lane = lax.broadcasted_iota(jnp.int32, v.shape, 1)
+    low = pltpu.roll(jnp.where(lane < EXPERTS, low.astype(f32), 0.0), EXPERTS, 1)
+    return (jnp.where(lane < EXPERTS, high.astype(f32), 0.0) + low).astype(bf16)
+
+
+def share_sum(t):
+    t = t.astype(f32)
+    lane = lax.broadcasted_iota(jnp.int32, t.shape, 1)
+    return jnp.where(lane < EXPERTS, t + pltpu.roll(t, PAD - EXPERTS, 1), 0.0)
+
+
 def join_kernel(keep, got, send, left):
     h = lax.axis_index("cuts") >> 1
     part = left.shape[1] - PAD
@@ -194,33 +210,15 @@
     v1 = keep[:, part : 2 * part] + got[:, part : 2 * part]
     share = keep[:, 2 * part :] + got[:, 2 * part :]
     left[:, :part] = jnp.where(h == 0, v0, v1)
-    send[:, :part] = jnp.where(h == 0, v1, v0)
+    send[:, :part] = jnp.where(h == 0, v1, v0).astype(bf16)
     left[:, part:] = share
-    send[:, part:] = share
-
-
-def stream_kernel(left, got, gate, up, out, gate_out, up_out):
+    send[:, part:] = share_parts(share)
+
+
+def stream_kernel(left, got, out):
     part = left.shape[1] - PAD
-    out[:, :part] = (left[:, :part] + got[:, :part]).astype(bf16)
-    high, low = halves(left[:, part:] + got[:, part:])
-    lane = lax.broadcasted_iota(jnp.int32, high.shape, 1)
-    low = pltpu.roll(jnp.where(lane < EXPERTS, low.astype(f32), 0.0), EXPERTS, 1)
-    out[:, part:] = (jnp.where(lane < EXPERTS, high.astype(f32), 0.0) + low).astype(bf16)
-
-
-def load_experts(experts, w_gate, w_up, outs, sem):
-    copies = []
-    for k, expert in enumerate(experts):
-        for w, out in ((w_gate, outs[2 * k]), (w_up, outs[2 * k + 1])):
-            at = pl.ds(pl.multiple_of(expert * FH, FH), FH)
-            n = len(copies)
-            step = w.shape[0] // SPLIT
-            for p in range(SPLIT):
-                rows = pl.ds(p * step, step)
-                copies.append(pltpu.make_async_copy(w.at[rows, at], out.at[rows], sem.at[n + p]))
-    for copy in copies:
-        copy.start()
-    return copies
+    out[:, :part] = (left[:, :part] + got[:, :part].astype(f32)).astype(bf16)
+    out[:, part:] = share_parts(left[:, part:] + share_sum(got[:, part:]))
 
 
 def expert_of(pair, other):
@@ -228,27 +226,24 @@
     return 2 * pair + (1 - b if other else b)
 
 
-def loads(which, part, after, w_gate, w_up, limit, held=()):
-    n, h = 2 * len(which), len(held)
-
-    def kernel(*refs):
-        sem = refs[-1]
-        copies = load_experts(
-            [expert_of(*w) for w in which], refs[h + 1], refs[h + 2], refs[2 * h + 3 : -1], sem
-        )
-        for copy in copies:
-            copy.wait()
-
-    return pl.pallas_call(
-        kernel,
-        in_specs=[VM] * h + [HB] * 3,
-        out_specs=[VM] * (h + n),
-        out_shape=[pltpu.VMEM((part, FH), bf16)] * (h + n),
-        input_output_aliases={i: i for i in range(h)},
-        scratch_shapes=[pltpu.SemaphoreType.DMA((SPLIT * n,))],
-        cost_estimate=QUICK,
-        compiler_params=pltpu.CompilerParams(vmem_limit_bytes=limit * MIB),
-    )(*held, after, w_gate, w_up)
+PIECES = ((0, True), (0, False), (1, True), (1, False))
+
+
+def load_kernel(w_up, after, w_gate, *refs):
+    gates, ups, sem = refs[:3], refs[3:7], refs[7]
+    copies = []
+    for w, outs, split in ((w_gate, gates, SPLIT), (w_up, ups, 1)):
+        for out, piece in zip(outs, PIECES):
+            at = pl.ds(pl.multiple_of(expert_of(*piece) * FH, FH), FH)
+            step = w.shape[0] // split
+            for p in range(split):
+                rows = pl.ds(p * step, step)
+                n = len(copies)
+                copies.append(pltpu.make_async_copy(w.at[rows, at], out.at[rows], sem.at[n]))
+    for copy in copies:
+        copy.start()
+    for copy in copies:
+        copy.wait()
 
 
 def load_down_kernel(after, w_down, *refs):
@@ -281,10 +276,7 @@
         at = pl.ds(k * rows_e, rows_e)
         x[at, :] = (v * weight).astype(bf16)
         square[at, :] = jnp.broadcast_to(jnp.sum(v * v, 1, keepdims=True), (rows_e, PAD))
-        t = s[:, part:].astype(f32)
-        lane = lax.broadcasted_iota(jnp.int32, t.shape, 1)
-        t = t + pltpu.roll(t, PAD - EXPERTS, 1)
-        share[at, :] = jnp.where(lane < EXPERTS, t, 0.0)
+        share[at, :] = share_sum(s[:, part:])
     expert_product(x, w_gate, w_up, send)
     send[:, 2 * FH :] = parts(square[...])
 
@@ -304,25 +296,23 @@
     expert_product(x, w_gate, w_up, out)
 
 
-def product_stream_kernel(x, gate_hbm, up_hbm, out, gate, up, sem):
-    expert = expert_of(1, False)
-    at = pl.ds(pl.multiple_of(expert * FH, FH), FH)
+def product_stream_kernel(x, up, gate_hbm, out, gate, sem):
+    at = pl.ds(pl.multiple_of(expert_of(1, False) * FH, FH), FH)
     step = 256
-    parts_of = x.shape[1] // step
     copies = []
-    for p in range(parts_of):
+    for p in range(x.shape[1] // step):
         rows = pl.ds(p * step, step)
-        for w, t in ((gate_hbm, gate), (up_hbm, up)):
-            copies.append(pltpu.make_async_copy(w.at[rows, at], t.at[rows], sem.at[len(copies)]))
+        copies.append(pltpu.make_async_copy(gate_hbm.at[rows, at], gate.at[rows], sem.at[p]))
     for copy in copies:
         copy.start()
-    for p in range(parts_of):
+    for i in range(FH // step):
+        to = pl.ds(i * step, step)
+        out[:, pl.ds(FH + i * step, step)] = jnp.dot(x[...], up[:, to], preferred_element_type=f32)
+    for p, copy in enumerate(copies):
         rows = pl.ds(p * step, step)
-        for k, t in enumerate((gate, up)):
-            copies[2 * p + k].wait()
-            v = jnp.dot(x[:, rows], t[rows, :], preferred_element_type=f32)
-            to = pl.ds(k * FH, FH)
-            out[:, to] = v if p == 0 else out[:, to] + v
+        copy.wait()
+        v = jnp.dot(x[:, rows], gate[rows, :], preferred_element_type=f32)
+        out[:, :FH] = v if p == 0 else out[:, :FH] + v
 
 
 def own_expert(pair):
@@ -402,7 +392,7 @@
             out[:, cols] = p
 
 
-def mixed_kernel(stream, own, r1, r2, r3, m0, m1, m2, m3):
+def mixed_kernel(stream, own, r3, r2, r1, m0, m1, m2, m3):
     c = lax.axis_index("cuts")
     part = own.shape[1]
     v = stream[:, :part].astype(f32) + own[...]
@@ -451,23 +441,14 @@
         ],
     )
     cut = (rows_e, part + PAD)
-    send, left = call(join_kernel, [(cut, f32)] * 2, keep, swap(send, "cuts", 1))
+    send, left = call(join_kernel, [(cut, bf16), (cut, f32)], keep, swap(send, "cuts", 1), cost=COVER)
     got = swap(send, "cuts", 2)
-    ga0, ua0 = loads([(0, True)], part, send, w_gate, w_up, 42)
-    s0, ga0, ua0 = pl.pallas_call(
-        stream_kernel,
-        in_specs=[VM] * 4,
-        out_specs=[VM] * 3,
-        out_shape=[jax.ShapeDtypeStruct(cut, bf16), weight, weight],
-        input_output_aliases={2: 1, 3: 2},
-        cost_estimate=QUICK,
-        compiler_params=pltpu.CompilerParams(vmem_limit_bytes=4 * MIB),
-    )(left, got, ga0, ua0)
+    (s0,) = call(stream_kernel, [(cut, bf16)], left, got, cost=COVER // 4)
     s3, s2, s1 = [swap(s0, "expert", k) for k in (3, 2, 1)]
-    ga0, ua0, gb0, ub0, ga1, ua1 = loads(
-        [(0, False), (1, True)], part, s0, w_gate, w_up, 29, (ga0, ua0)
-    )
-
+    ga0, gb0, ga1, ua0, ub0, ua1, ub1 = call(
+        load_kernel, [weight] * 7, w_up, s0, w_gate, far=2, limit=4,
+        scratch=[pltpu.SemaphoreType.DMA((3 * SPLIT + 4,))],
+    )
     x, send, share, square = call(
         first_kernel,
         [((rows, part), bf16), ((rows, 2 * FH + PAD), bf16), ((rows, PAD), f32), ((rows, PAD), f32)],
@@ -488,11 +469,8 @@
     (send,) = call(product_kernel, [sent_all], x, ga1, ua1)
     got = swap(send, "cuts", 1)
     (keep,) = call(
-        product_stream_kernel, [full], x, w_gate, w_up, far=2, limit=40,
-        scratch=[
-            pltpu.VMEM((part, FH), bf16), pltpu.VMEM((part, FH), bf16),
-            pltpu.SemaphoreType.DMA((2 * (part // 256),)),
-        ],
+        product_stream_kernel, [full], x, ub1, w_gate, far=1, limit=47,
+        scratch=[pltpu.VMEM((part, FH), bf16), pltpu.SemaphoreType.DMA((part // 256,))],
     )
     total1, send, place1 = call(
         functools.partial(sum_kernel, own_rows), [full, sent, place], keep, got, square, share
@@ -504,7 +482,7 @@
         out_specs=[VM] * 5,
         out_shape=[pltpu.VMEM((FH, part), bf16)] * 4 + [jax.ShapeDtypeStruct((8, PAD), f32)],
         scratch_shapes=[pltpu.SemaphoreType.DMA((4,))],
-        cost_estimate=QUICK,
+        cost_estimate=pl.CostEstimate(flops=1, bytes_accessed=1, transcendentals=0),
         compiler_params=pltpu.CompilerParams(vmem_limit_bytes=34 * MIB),
     )(send, w_down)
 
@@ -529,7 +507,7 @@
         g1, d3, t,
     )
     r3, r2, r1 = [swap(o, "expert", k) for k, o in ((3, o3), (2, o2), (1, o1))]
-    m0, m1, m2, m3 = call(mixed_kernel, [((own_rows, part), bf16)] * 4, s0, o0, r1, r2, r3)
+    m0, m1, m2, m3 = call(mixed_kernel, [((own_rows, part), bf16)] * 4, s0, o0, r3, r2, r1)
     m2, m3, m1 = [swap(m, "cuts", k) for k, m in ((2, m2), (3, m3), (1, m1))]
     (mixed,) = call(final_kernel, [((own_rows, width), bf16)], m0, m1, m2, m3)
     return mixed

time: 56.6 us -> 52.7 us (0.931)
  Pallas kernels: 28.2 us -> 22.9 us
  waiting for transfers between devices: 10.9 us -> 12 us
    pallas_call x3 -> x0, Pallas kernels: 8.65 us -> none  [the longest x2 8.57 us: loads(): pl.pallas_call(kernel, in_specs=[VM] * h + [HB] * 3, out_specs=[VM] * (h...]
    pallas_call x16 -> x18, Pallas kernels: 14.3 us -> 17.7 us  [call(): pl.pallas_call(kernel, in_specs=[VM] * (len(args) - far) + [HB] * far, ou...]
    ppermute x17, waiting for transfers between devices: 10.9 us -> 12 us  [swap(): return lax.ppermute(x, axis, [(i, i ^ bit) for i in range(n)])]
  transfers between devices with their start and end apart: 17 -> 17, of which waited for: 8 -> 9; matrix products, arithmetic and copies ran while one was open for 0% -> 0% of each run, Pallas kernels for 42% -> 35%
where the time goes in v3:
time: 52.7 us; the launch traced here: 52.6 us
  Pallas kernels  22.9 us (43%)
  starting transfers between devices  17.4 us (33%)
  waiting for transfers between devices  12 us (23%)
    pallas_call x18, Pallas kernels, call(): pl.pallas_call(kernel, in_specs=[VM] * (len(args) - far) + [HB] * far, ou...  17.7 us
    ppermute x17, starting transfers between devices, swap(): return lax.ppermute(x, axis, [(i, i ^ bit) for i in range(n)])  17.4 us
    ppermute x17, waiting for transfers between devices, swap(): return lax.ppermute(x, axis, [(i, i ^ bit) for i in range(n)])  12 us
    pallas_call x1, Pallas kernels, fast_body(): pl.pallas_call(load_down_kernel, in_specs=[HB] * 2, out_specs=[VM] * 5, o...  5.28 us
  transfers between devices with their start and end apart: 17, of which 9 were waited for; matrix products, arithmetic and copies ran while one was open for 0% of the time, Pallas kernels for 35%

profile of v3, /device:TPU:0, one launch (start us, length us, event | category | flops | bytes accessed | tf_op | source)
XLA Modules:
  0.0 52.6 jit_solution(2124180166034718895)
XLA Ops:
  0.0 1.2 %shard_map.91 = (f32[16,3712]{1,0:T(8,128)S(1)}, f32[16,3712]{1,0:T(8,128)S(1)}, f32[1,1792]{1,0:T(1,128)S(1)}, f32[1,16]{1,0:T(1,128)S(1)}) custom-call(f32[1,16,7168]{2,1,0:T(8,128)} %refs_0_.1, bf16[4,7168]{1,0:T(4,128)(2,1)} %refs_1_.1, s32[4,8]{1,0:T(4,128)} %refs_2_.1, f32[4,8]{1,0:T(4,128)} %refs_3_.1, f32[56,128]{1,0:T(8,128)} %bitcast.2, ...), custom_call_target="tpu_custom_call" | custom-call | flops 1 | bytes 1 | tf_op jit(solution)/shard_map/pallas_call | solution.py:124
  1.7 1.1 %collective-permute-done.got = f32[16,3712]{1,0:T(8,128)S(1)} collective-permute-done((f32[16,3712]{1,0:T(8,128)S(1)}, f32[16,3712]{1,0:T(8,128)S(1)}, u32[]{:S(2)}, u32[]{:S(2)}) %collective-permute-start) | collective-permute-done | bytes 237600 | tf_op jit(solution)/shard_map/ppermute | solution.py:24
  2.9 2.9 %collective-permute-start.1 = (bf16[16,1920]{1,0:T(8,128)(2,1)S(1)}, bf16[16,1920]{1,0:T(8,128)(2,1)S(1)}, u32[]{:S(2)}, u32[]{:S(2)}) collective-permute-start(bf16[16,1920]{1,0:T(8,128)(2,1)S(1)} %get-tuple-element.45), channel_id=1, source_target_pairs={{0,2},{1,3},{2,0},{3,1},{4,6},{5,7},{6,4},{7,5},{8,10},{9,11},{10,... | collective-permute-start | bytes 184328 | tf_op jit(solution)/shard_map/ppermute | solution.py:24
  5.8 2.3 %collective-permute-done.1.got = bf16[16,1920]{1,0:T(8,128)(2,1)S(1)} collective-permute-done((bf16[16,1920]{1,0:T(8,128)(2,1)S(1)}, bf16[16,1920]{1,0:T(8,128)(2,1)S(1)}, u32[]{:S(2)}, u32[]{:S(2)}) %collective-permute-start.1) | collective-permute-done | bytes 61472 | tf_op jit(solution)/shard_map/ppermute | solution.py:24
  8.3 4.0 %collective-permute-start.4 = (bf16[16,1920]{1,0:T(8,128)(2,1)S(1)}, bf16[16,1920]{1,0:T(8,128)(2,1)S(1)}, u32[]{:S(2)}, u32[]{:S(2)}) collective-permute-start(bf16[16,1920]{1,0:T(8,128)(2,1)S(1)} %shard_map.93.after.s0.stream), channel_id=1, source_target_pairs={{0,12},{4,8},{8,4},{12,0},{1,13},{5,9},{9,5},{13,1},{2,14},{6,10},... | collective-permute-start | bytes 184328 | tf_op jit(solution)/shard_map/ppermute | solution.py:24
  12.9 4.3 %shard_map.94 = (bf16[1792,1024]{1,0:T(8,128)(2,1)S(1)}, bf16[1792,1024]{1,0:T(8,128)(2,1)S(1)}, bf16[1792,1024]{1,0:T(8,128)(2,1)S(1)}, bf16[1792,1024]{1,0:T(8...) custom-call(bf16[1792,4096]{1,0:T(8,128)(2,1)S(1)} %copy-done, ...), custom_call_target="tpu_custom_call" | custom-call | flops 1 | bytes 1 | tf_op jit(solution)/shard_map/pallas_call | solution.py:124
  17.6 1.4 %shard_map.95 = (bf16[64,1792]{1,0:T(8,128)(2,1)S(1)}, bf16[64,2176]{1,0:T(8,128)(2,1)S(1)}, f32[64,128]{1,0:T(8,128)S(1)}, f32[64,128]{1,0:T(8,128)S(1)}) custom-call(bf16[16,1920]{1,0:T(8,128)(2,1)S(1)} %shard_map.93.after.s0.stream, bf16[16,1920]{1,0:T(8,128)(2,1)S(1)} %collective-permute-done.2.s1, bf16[16,1920]{1,0:T(8,128)(2,1)S(1)} %collective-permute-done.3.s2, ...), custom_call_target="tpu_custom_call" | custom-call | flops 1 | bytes 1 | tf_op jit(solution)/shard_map/pallas_call | solution.py:124
  19.1 1.4 %shard_map.97 = bf16[64,2048]{1,0:T(8,128)(2,1)S(1)} custom-call(bf16[64,1792]{1,0:T(8,128)(2,1)S(1)} %get-tuple-element.49.x, bf16[1792,1024]{1,0:T(8,128)(2,1)S(1)} %get-tuple-element.51.w_gate, bf16[1792,1024]{1,0:T(8,128)(2,1)S(1)} %get-tuple-element.52.w_up), custom_call_target="tpu_custom_call" | custom-call | flops 1 | bytes 1 | tf_op jit(solution)/shard_map/pallas_call | solution.py:124
  21.0 1.4 %shard_map.98.keep = f32[64,2048]{1,0:T(8,128)S(1)} custom-call(bf16[64,1792]{1,0:T(8,128)(2,1)S(1)} %get-tuple-element.49.x, bf16[1792,1024]{1,0:T(8,128)(2,1)S(1)} %get-tuple-element.53.w_gate, bf16[1792,1024]{1,0:T(8,128)(2,1)S(1)} %get-tuple-element.54.w_up), custom_call_target="tpu_custom_call" | custom-call | flops 1 | bytes 1 | tf_op jit(solution)/shard_map/pallas_call | solution.py:124
  22.9 1.6 %collective-permute-start.9 = (bf16[48,2176]{1,0:T(8,128)(2,1)S(1)}, bf16[48,2176]{1,0:T(8,128)(2,1)S(1)}, u32[]{:S(2)}, u32[]{:S(2)}) collective-permute-start(bf16[48,2176]{1,0:T(8,128)(2,1)S(1)} %get-tuple-element.67), channel_id=1, source_target_pairs={{0,2},{1,3},{2,0},{3,1},{4,6},{5,7},{6,4},{7,5},{8,10},{9,11},{10,... | collective-permute-start | bytes 626696 | tf_op jit(solution)/shard_map/ppermute | solution.py:24
  24.4 2.3 %shard_map.96.keep = f32[64,2048]{1,0:T(8,128)S(1)} custom-call(bf16[64,1792]{1,0:T(8,128)(2,1)S(1)} %get-tuple-element.49.x, bf16[1792,1024]{1,0:T(8,128)(2,1)S(1)} %get-tuple-element.50.up, bf16[1792,4096]{1,0:T(8,128)(2,1)} %gate_hbm.1), custom_call_target="tpu_custom_call" | custom-call | flops 1 | bytes 1 | tf_op jit(solution)/shard_map/pallas_call | solution.py:124
  27.8 5.3 %shard_map.101 = (bf16[1024,1792]{1,0:T(8,128)(2,1)S(1)}, bf16[1024,1792]{1,0:T(8,128)(2,1)S(1)}, bf16[1024,1792]{1,0:T(8,128)(2,1)S(1)}, bf16[1024,1792]{1,0:T(8,128)(2,1)S(1)}, f32[8,128]{1,0:T(8,128)S(1)}) custom-call(bf16[48,2176]{1,0:T(8,128)(2,1)S(1)} %get-tuple-element.60.after, bf16[4096,1792]{1,0:T(8,128)(2,1)} %w_down.1), custom_call_target="tpu_custom_call" | custom-call | flops 1 | bytes 1 | tf_op jit(solution)/shard_map/pallas_call | solution.py:479
  33.6 1.0 %collective-permute-done.7.got = bf16[48,2176]{1,0:T(8,128)(2,1)S(1)} collective-permute-done((bf16[48,2176]{1,0:T(8,128)(2,1)S(1)}, bf16[48,2176]{1,0:T(8,128)(2,1)S(1)}, u32[]{:S(2)}, u32[]{:S(2)}) %collective-permute-start.7) | collective-permute-done | bytes 208928 | tf_op jit(solution)/shard_map/ppermute | solution.py:24
  35.0 0.8 %shard_map.104.refs_2_ = f32[64,1792]{1,0:T(8,128)S(1)} custom-call(bf16[64,1024]{1,0:T(8,128)(2,1)S(1)} %shard_map.103.refs_0_, bf16[1024,1792]{1,0:T(8,128)(2,1)S(1)} %get-tuple-element.70.refs_1_), custom_call_target="tpu_custom_call" | custom-call | flops 1 | bytes 1 | tf_op jit(solution)/shard_map/pallas_call | solution.py:124
  35.8 0.8 %shard_map.105.refs_2_ = f32[64,1792]{1,0:T(8,128)S(1)} custom-call(bf16[64,1024]{1,0:T(8,128)(2,1)S(1)} %collective-permute-done.10.refs_0_, bf16[1024,1792]{1,0:T(8,128)(2,1)S(1)} %get-tuple-element.69.refs_1_, f32[64,1792]{1,0:T(8,128)S(1)} %shard_map.104.refs_2_), custom_call_target="tpu_custom_call" | custom-call | flops 1 | bytes 1 | tf_op jit(solution)/shard_map/pallas_call | solution.py:124
  36.5 0.8 %shard_map.106.refs_2_ = f32[64,1792]{1,0:T(8,128)S(1)} custom-call(bf16[64,1024]{1,0:T(8,128)(2,1)S(1)} %shard_map.102.refs_0_, bf16[1024,1792]{1,0:T(8,128)(2,1)S(1)} %get-tuple-element.65.refs_1_, f32[64,1792]{1,0:T(8,128)S(1)} %shard_map.105.refs_2_), custom_call_target="tpu_custom_call" | custom-call | flops 1 | bytes 1 | tf_op jit(solution)/shard_map/pallas_call | solution.py:124
  37.3 0.8 %shard_map.107 = (f32[16,1792]{1,0:T(8,128)S(1)}, bf16[16,1792]{1,0:T(8,128)(2,1)S(1)}, bf16[16,1792]{1,0:T(8,128)(2,1)S(1)}, bf16[16,1792]{1,0:T(8,128)(2,1)S(1)}) custom-call(bf16[64,1024]{1,0:T(8,128)(2,1)S(1)} %collective-permute-done.8.refs_0_, bf16[1024,1792]{1,0:T(8,128)(2,1)S(1)} %get-tuple-element.64.refs_1_, f32[64,1792]{1,0:T(8,128)S(1)} %shard_map.106.refs_2_), custom_call_target="tpu_custom_call" | custom-call | flops 1 | bytes 1 | tf_op jit(solution)/shard_map/pallas_call | solution.py:124
  38.1 3.5 %collective-permute-start.11 = (bf16[16,1792]{1,0:T(8,128)(2,1)S(1)}, bf16[16,1792]{1,0:T(8,128)(2,1)S(1)}, u32[]{:S(2)}, u32[]{:S(2)}) collective-permute-start(bf16[16,1792]{1,0:T(8,128)(2,1)S(1)} %get-tuple-element.72), channel_id=1, source_target_pairs={{0,12},{4,8},{8,4},{12,0},{1,13},{5,9},{9,5},{13,1},{2,14},{6,10},... | collective-permute-start | bytes 172040 | tf_op jit(solution)/shard_map/ppermute | solution.py:24
  41.7 0.9 %collective-permute-start.13 = (bf16[16,1792]{1,0:T(8,128)(2,1)S(1)}, bf16[16,1792]{1,0:T(8,128)(2,1)S(1)}, u32[]{:S(2)}, u32[]{:S(2)}) collective-permute-start(bf16[16,1792]{1,0:T(8,128)(2,1)S(1)} %get-tuple-element.74), channel_id=1, source_target_pairs={{0,4},{4,0},{8,12},{12,8},{1,5},{5,1},{9,13},{13,9},{2,6},{6,2},{1... | collective-permute-start | bytes 172040 | tf_op jit(solution)/shard_map/ppermute | solution.py:24
  42.6 2.1 %collective-permute-done.11.r3 = bf16[16,1792]{1,0:T(8,128)(2,1)S(1)} collective-permute-done((bf16[16,1792]{1,0:T(8,128)(2,1)S(1)}, bf16[16,1792]{1,0:T(8,128)(2,1)S(1)}, u32[]{:S(2)}, u32[]{:S(2)}) %collective-permute-start.11) | collective-permute-done | bytes 57376 | tf_op jit(solution)/shard_map/ppermute | solution.py:24
  44.7 2.2 %collective-permute-done.12.r2 = bf16[16,1792]{1,0:T(8,128)(2,1)S(1)} collective-permute-done((bf16[16,1792]{1,0:T(8,128)(2,1)S(1)}, bf16[16,1792]{1,0:T(8,128)(2,1)S(1)}, u32[]{:S(2)}, u32[]{:S(2)}) %collective-permute-start.12) | collective-permute-done | bytes 57376 | tf_op jit(solution)/shard_map/ppermute | solution.py:24
  47.2 1.6 %collective-permute-start.15 = (bf16[4,1792]{1,0:T(4,128)(2,1)S(1)}, bf16[4,1792]{1,0:T(4,128)(2,1)S(1)}, u32[]{:S(2)}, u32[]{:S(2)}) collective-permute-start(bf16[4,1792]{1,0:T(4,128)(2,1)S(1)} %get-tuple-element.77), channel_id=1, source_target_pairs={{0,2},{1,3},{2,0},{3,1},{4,6},{5,7},{6,4},{7,5},{8,10},{9,11},{10,... | collective-permute-start | bytes 43016 | tf_op jit(solution)/shard_map/ppermute | solution.py:24
  49.1 1.9 %collective-permute-done.15.m2 = bf16[4,1792]{1,0:T(4,128)(2,1)S(1)} collective-permute-done((bf16[4,1792]{1,0:T(4,128)(2,1)S(1)}, bf16[4,1792]{1,0:T(4,128)(2,1)S(1)}, u32[]{:S(2)}, u32[]{:S(2)}) %collective-permute-start.15) | collective-permute-done | bytes 14368 | tf_op jit(solution)/shard_map/ppermute | solution.py:24
  51.0 0.9 %collective-permute-done.16.m3 = bf16[4,1792]{1,0:T(4,128)(2,1)S(1)} collective-permute-done((bf16[4,1792]{1,0:T(4,128)(2,1)S(1)}, bf16[4,1792]{1,0:T(4,128)(2,1)S(1)}, u32[]{:S(2)}, u32[]{:S(2)}) %collective-permute-start.16) | collective-permute-done | bytes 14368 | tf_op jit(solution)/shard_map/ppermute | solution.py:24
  (31 shorter events, 6.0 us)
Async XLA Ops:
  1.2 1.6 %collective-permute-start = (f32[16,3712]{1,0:T(8,128)S(1)}, f32[16,3712]{1,0:T(8,128)S(1)}, u32[]{:S(2)}, u32[]{:S(2)}) collective-permute-start(f32[16,3712]{1,0:T(8,128)S(1)} %get-tuple-element.43), channel_id=1, source_target_pairs={{0,1},{1,0},{2,3},{3,2},{4,5},{5,4},{6,7},{7,6},{8,9},{9,8},{10,11... | collective-permute-start | bytes 712712 | tf_op jit(solution)/shard_map/ppermute | solution.py:24
  2.8 10.1 %copy-start = (bf16[1792,4096]{1,0:T(8,128)(2,1)S(1)}, bf16[1792,4096]{1,0:T(8,128)(2,1)}, u32[]{:S(2)}) copy-start(bf16[1792,4096]{1,0:T(8,128)(2,1)} %w_up.1) | copy-start | bytes 44040196
  2.9 5.2 %collective-permute-start.1 = (bf16[16,1920]{1,0:T(8,128)(2,1)S(1)}, bf16[16,1920]{1,0:T(8,128)(2,1)S(1)}, u32[]{:S(2)}, u32[]{:S(2)}) collective-permute-start(bf16[16,1920]{1,0:T(8,128)(2,1)S(1)} %get-tuple-element.45), channel_id=1, source_target_pairs={{0,2},{1,3},{2,0},{3,1},{4,6},{5,7},{6,4},{7,5},{8,10},{9,11},{10,... | collective-permute-start | bytes 184328 | tf_op jit(solution)/shard_map/ppermute | solution.py:24
  8.3 9.0 %collective-permute-start.4 = (bf16[16,1920]{1,0:T(8,128)(2,1)S(1)}, bf16[16,1920]{1,0:T(8,128)(2,1)S(1)}, u32[]{:S(2)}, u32[]{:S(2)}) collective-permute-start(bf16[16,1920]{1,0:T(8,128)(2,1)S(1)} %shard_map.93.after.s0.stream), channel_id=1, source_target_pairs={{0,12},{4,8},{8,4},{12,0},{1,13},{5,9},{9,5},{13,1},{2,14},{6,10},... | collective-permute-start | bytes 184328 | tf_op jit(solution)/shard_map/ppermute | solution.py:24
  12.3 5.3 %collective-permute-start.3 = (bf16[16,1920]{1,0:T(8,128)(2,1)S(1)}, bf16[16,1920]{1,0:T(8,128)(2,1)S(1)}, u32[]{:S(2)}, u32[]{:S(2)}) collective-permute-start(bf16[16,1920]{1,0:T(8,128)(2,1)S(1)} %shard_map.93.after.s0.stream), channel_id=1, source_target_pairs={{0,8},{4,12},{8,0},{12,4},{1,9},{5,13},{9,1},{13,5},{2,10},{6,14},... | collective-permute-start | bytes 184328 | tf_op jit(solution)/shard_map/ppermute | solution.py:24
  12.3 5.3 %collective-permute-start.2 = (bf16[16,1920]{1,0:T(8,128)(2,1)S(1)}, bf16[16,1920]{1,0:T(8,128)(2,1)S(1)}, u32[]{:S(2)}, u32[]{:S(2)}) collective-permute-start(bf16[16,1920]{1,0:T(8,128)(2,1)S(1)} %shard_map.93.after.s0.stream), channel_id=1, source_target_pairs={{0,4},{4,0},{8,12},{12,8},{1,5},{5,1},{9,13},{13,9},{2,6},{6,2},{1... | collective-permute-start | bytes 184328 | tf_op jit(solution)/shard_map/ppermute | solution.py:24
  19.0 3.5 %collective-permute-start.6 = (bf16[64,2176]{1,0:T(8,128)(2,1)S(1)}, bf16[64,2176]{1,0:T(8,128)(2,1)S(1)}, u32[]{:S(2)}, u32[]{:S(2)}) collective-permute-start(bf16[64,2176]{1,0:T(8,128)(2,1)S(1)} %get-tuple-element.55), channel_id=1, source_target_pairs={{0,1},{1,0},{2,3},{3,2},{4,5},{5,4},{6,7},{7,6},{8,9},{9,8},{10,11... | collective-permute-start | bytes 835592 | tf_op jit(solution)/shard_map/ppermute | solution.py:24
  20.5 6.3 %collective-permute-start.5 = (bf16[64,2048]{1,0:T(8,128)(2,1)S(1)}, bf16[64,2048]{1,0:T(8,128)(2,1)S(1)}, u32[]{:S(2)}, u32[]{:S(2)}) collective-permute-start(bf16[64,2048]{1,0:T(8,128)(2,1)S(1)} %shard_map.97), channel_id=1, source_target_pairs={{0,1},{1,0},{2,3},{3,2},{4,5},{5,4},{6,7},{7,6},{8,9},{9,8},{10,11... | collective-permute-start | bytes 786440 | tf_op jit(solution)/shard_map/ppermute | solution.py:24
  22.9 10.2 %collective-permute-start.9 = (bf16[48,2176]{1,0:T(8,128)(2,1)S(1)}, bf16[48,2176]{1,0:T(8,128)(2,1)S(1)}, u32[]{:S(2)}, u32[]{:S(2)}) collective-permute-start(bf16[48,2176]{1,0:T(8,128)(2,1)S(1)} %get-tuple-element.67), channel_id=1, source_target_pairs={{0,2},{1,3},{2,0},{3,1},{4,6},{5,7},{6,4},{7,5},{8,10},{9,11},{10,... | collective-permute-start | bytes 626696 | tf_op jit(solution)/shard_map/ppermute | solution.py:24
  27.2 7.3 %collective-permute-start.7 = (bf16[48,2176]{1,0:T(8,128)(2,1)S(1)}, bf16[48,2176]{1,0:T(8,128)(2,1)S(1)}, u32[]{:S(2)}, u32[]{:S(2)}) collective-permute-start(bf16[48,2176]{1,0:T(8,128)(2,1)S(1)} %get-tuple-element.60.after), channel_id=1, source_target_pairs={{0,2},{1,3},{2,0},{3,1},{4,6},{5,7},{6,4},{7,5},{8,10},{9,11},{10,... | collective-permute-start | bytes 626696 | tf_op jit(solution)/shard_map/ppermute | solution.py:24
  33.5 2.3 %collective-permute-start.10 = (bf16[64,1024]{1,0:T(8,128)(2,1)S(1)}, bf16[64,1024]{1,0:T(8,128)(2,1)S(1)}, u32[]{:S(2)}, u32[]{:S(2)}) collective-permute-start(bf16[64,1024]{1,0:T(8,128)(2,1)S(1)} %shard_map.103.refs_0_), channel_id=1, source_target_pairs={{0,1},{1,0},{2,3},{3,2},{4,5},{5,4},{6,7},{7,6},{8,9},{9,8},{10,11... | collective-permute-start | bytes 393224 | tf_op jit(solution)/shard_map/ppermute | solution.py:24
  34.9 2.4 %collective-permute-start.8 = (bf16[64,1024]{1,0:T(8,128)(2,1)S(1)}, bf16[64,1024]{1,0:T(8,128)(2,1)S(1)}, u32[]{:S(2)}, u32[]{:S(2)}) collective-permute-start(bf16[64,1024]{1,0:T(8,128)(2,1)S(1)} %shard_map.102.refs_0_), channel_id=1, source_target_pairs={{0,1},{1,0},{2,3},{3,2},{4,5},{5,4},{6,7},{7,6},{8,9},{9,8},{10,11... | collective-permute-start | bytes 393224 | tf_op jit(solution)/shard_map/ppermute | solution.py:24
  38.1 6.6 %collective-permute-start.11 = (bf16[16,1792]{1,0:T(8,128)(2,1)S(1)}, bf16[16,1792]{1,0:T(8,128)(2,1)S(1)}, u32[]{:S(2)}, u32[]{:S(2)}) collective-permute-start(bf16[16,1792]{1,0:T(8,128)(2,1)S(1)} %get-tuple-element.72), channel_id=1, source_target_pairs={{0,12},{4,8},{8,4},{12,0},{1,13},{5,9},{9,5},{13,1},{2,14},{6,10},... | collective-permute-start | bytes 172040 | tf_op jit(solution)/shard_map/ppermute | solution.py:24
  41.7 5.2 %collective-permute-start.12 = (bf16[16,1792]{1,0:T(8,128)(2,1)S(1)}, bf16[16,1792]{1,0:T(8,128)(2,1)S(1)}, u32[]{:S(2)}, u32[]{:S(2)}) collective-permute-start(bf16[16,1792]{1,0:T(8,128)(2,1)S(1)} %get-tuple-element.73), channel_id=1, source_target_pairs={{0,8},{4,12},{8,0},{12,4},{1,9},{5,13},{9,1},{13,5},{2,10},{6,14},... | collective-permute-start | bytes 172040 | tf_op jit(solution)/shard_map/ppermute | solution.py:24
  41.7 5.4 %collective-permute-start.13 = (bf16[16,1792]{1,0:T(8,128)(2,1)S(1)}, bf16[16,1792]{1,0:T(8,128)(2,1)S(1)}, u32[]{:S(2)}, u32[]{:S(2)}) collective-permute-start(bf16[16,1792]{1,0:T(8,128)(2,1)S(1)} %get-tuple-element.74), channel_id=1, source_target_pairs={{0,4},{4,0},{8,12},{12,8},{1,5},{5,1},{9,13},{13,9},{2,6},{6,2},{1... | collective-permute-start | bytes 172040 | tf_op jit(solution)/shard_map/ppermute | solution.py:24
  47.1 1.9 %collective-permute-start.14 = (bf16[4,1792]{1,0:T(4,128)(2,1)S(1)}, bf16[4,1792]{1,0:T(4,128)(2,1)S(1)}, u32[]{:S(2)}, u32[]{:S(2)}) collective-permute-start(bf16[4,1792]{1,0:T(4,128)(2,1)S(1)} %get-tuple-element.76), channel_id=1, source_target_pairs={{0,1},{1,0},{2,3},{3,2},{4,5},{5,4},{6,7},{7,6},{8,9},{9,8},{10,11... | collective-permute-start | bytes 43016 | tf_op jit(solution)/shard_map/ppermute | solution.py:24
  47.2 3.8 %collective-permute-start.15 = (bf16[4,1792]{1,0:T(4,128)(2,1)S(1)}, bf16[4,1792]{1,0:T(4,128)(2,1)S(1)}, u32[]{:S(2)}, u32[]{:S(2)}) collective-permute-start(bf16[4,1792]{1,0:T(4,128)(2,1)S(1)} %get-tuple-element.77), channel_id=1, source_target_pairs={{0,2},{1,3},{2,0},{3,1},{4,6},{5,7},{6,4},{7,5},{8,10},{9,11},{10,... | collective-permute-start | bytes 43016 | tf_op jit(solution)/shard_map/ppermute | solution.py:24
  48.8 3.1 %collective-permute-start.16 = (bf16[4,1792]{1,0:T(4,128)(2,1)S(1)}, bf16[4,1792]{1,0:T(4,128)(2,1)S(1)}, u32[]{:S(2)}, u32[]{:S(2)}) collective-permute-start(bf16[4,1792]{1,0:T(4,128)(2,1)S(1)} %get-tuple-element.78), channel_id=1, source_target_pairs={{0,3},{1,2},{2,1},{3,0},{4,7},{5,6},{6,5},{7,4},{8,11},{9,10},{10,... | collective-permute-start | bytes 43016 | tf_op jit(solution)/shard_map/ppermute | solution.py:24

commit v4 on v3

--- a/solution.py
+++ b/solution.py
@@ -339,30 +339,42 @@
     return lax.dot_general(where, v, dims, preferred_element_type=f32).astype(bf16)
 
 
-def payload(v, square, share, pair, own_rows, send, place):
+def payload(v, share, pair, own_rows, send, place):
     where = places(column(share[...], own_expert(pair)), own_rows, send.shape[0])
     place[...] = where
     send[:, : 2 * FH] = packed(v.astype(bf16), where)
-    send[:, 2 * FH :] = packed(parts(square), where)
+
+
+def lanes(shape):
+    lane = lax.broadcasted_iota(jnp.int32, shape, 1)
+    row = lax.broadcasted_iota(jnp.int32, shape, 0)
+    return lane == row, lane == row + shape[0]
 
 
 def first_sum_kernel(own_rows, keep, got, square, share, total, send, square_out, place):
     v = keep[...] + got[:, : 2 * FH].astype(f32)
     total[...] = v
+    payload(v, share, 0, own_rows, send, place)
     s = square[...] + pair_sum(got[:, 2 * FH :].astype(f32))
     square_out[...] = s
-    payload(v, s, share, 0, own_rows, send, place)
-
-
-def sum_kernel(own_rows, keep, got, square, share, total, send, place):
+    high, low = halves(s)
+    at_high, at_low = lanes(s.shape)
+    t = jnp.where(at_high, high.astype(f32), jnp.where(at_low, low.astype(f32), 0.0))
+    t = jnp.broadcast_to(jnp.sum(t, 0, keepdims=True), (send.shape[0], PAD))
+    send[:, 2 * FH :] = t.astype(bf16)
+
+
+def sum_kernel(own_rows, keep, got, share, total, send, place):
     v = keep[...] + got[...].astype(f32)
     total[...] = v
-    payload(v, square[...], share, 1, own_rows, send, place)
-
-
-def hidden_kernel(pair, width, total, got, square, place, share, scale, after, out):
-    squares = pair_sum(jnp.dot(place[...], got[:, 2 * FH :], preferred_element_type=f32))
-    factor = lax.rsqrt((square[...] + squares) / width + 1e-06)[:, :1]
+    payload(v, share, 1, own_rows, send, place)
+
+
+def hidden_kernel(pair, width, total, got, first, square, place, share, scale, after, out):
+    at_high, at_low = lanes(square.shape)
+    t = jnp.broadcast_to(first[:16, 2 * FH :].astype(f32)[:1], square.shape)
+    squares = square[:, :1] + jnp.sum(jnp.where(at_high | at_low, t, 0.0), 1, keepdims=True)
+    factor = lax.rsqrt(squares / width + 1e-06)
     expert = own_expert(pair)
     coefficient = column(share[...], expert) * column(scale[...], expert)
     v = jnp.dot(place[...], got[:, : 2 * FH], preferred_element_type=f32)
@@ -473,7 +485,7 @@
         scratch=[pltpu.VMEM((part, FH), bf16), pltpu.SemaphoreType.DMA((part // 256,))],
     )
     total1, send, place1 = call(
-        functools.partial(sum_kernel, own_rows), [full, sent, place], keep, got, square, share
+        functools.partial(sum_kernel, own_rows), [full, ((slots, 2 * FH), bf16), place], keep, got, share
     )
     got1 = swap(send, "cuts", 2)
     d0, d1, d2, d3, after = pl.pallas_call(
@@ -490,15 +502,15 @@
     out = ((rows, part), f32)
     (h0,) = call(
         functools.partial(hidden_kernel, 0, width), [half],
-        total0, got0, square, place0, share, scale, after,
+        total0, got0, got0, square, place0, share, scale, after,
     )
     g0 = swap(h0, "cuts", 1)
     (t,) = call(functools.partial(down_kernel, False), [out], h0, d0)
-    (t,) = call(functools.partial(down_kernel, False), [out], g0, d1, t)
     (h1,) = call(
         functools.partial(hidden_kernel, 1, width), [half],
-        total1, got1, square, place1, share, scale, after,
-    )
+        total1, got1, got0, square, place1, share, scale, t, far=1,
+    )
+    (t,) = call(functools.partial(down_kernel, False), [out], g0, d1, t)
     g1 = swap(h1, "cuts", 1)
     (t,) = call(functools.partial(down_kernel, False), [out], h1, d2, t)
     o0, o1, o2, o3 = call(
@@ -527,6 +539,11 @@
     )
     out_specs = P(("group", "expert", "cuts"), None)
     small = mesh.shape["expert"] == 4 and mesh.shape["cuts"] == 4
+
+    def pick_body(*args):
+        fits = small and 32 * args[0].shape[0] <= PAD
+        return (fast_body if fits else body)(*args)
+
     return jax.shard_map(
-        fast_body if small else body, mesh=mesh, in_specs=in_specs, out_specs=out_specs, check_vma=False
-    )
+        pick_body, mesh=mesh, in_specs=in_specs, out_specs=out_specs, check_vma=False
+    )

time: 52.7 us -> 52 us (0.987)
  waiting for transfers between devices: 12 us -> 11.1 us
    ppermute x17, waiting for transfers between devices: 12 us -> 11.1 us  [swap(): return lax.ppermute(x, axis, [(i, i ^ bit) for i in range(n)])]
  transfers between devices with their start and end apart: 17 -> 17, of which waited for: 9 -> 8; matrix products, arithmetic and copies ran while one was open for 0% -> 0% of each run, Pallas kernels for 35% -> 35%
where the time goes in v4:
time: 52 us; the launch traced here: 51.8 us
  Pallas kernels  22.7 us (44%)
  starting transfers between devices  17.9 us (34%)
  waiting for transfers between devices  11.1 us (21%)
    ppermute x17, starting transfers between devices, swap(): return lax.ppermute(x, axis, [(i, i ^ bit) for i in range(n)])  17.9 us
    pallas_call x18, Pallas kernels, call(): pl.pallas_call(kernel, in_specs=[VM] * (len(args) - far) + [HB] * far, ou...  17.4 us
    ppermute x17, waiting for transfers between devices, swap(): return lax.ppermute(x, axis, [(i, i ^ bit) for i in range(n)])  11.1 us
    pallas_call x1, Pallas kernels, fast_body(): pl.pallas_call(load_down_kernel, in_specs=[HB] * 2, out_specs=[VM] * 5, o...  5.28 us
  transfers between devices with their start and end apart: 17, of which 8 were waited for; matrix products, arithmetic and copies ran while one was open for 0% of the time, Pallas kernels for 35%

profile of v4, /device:TPU:0, one launch (start us, length us, event | category | flops | bytes accessed | tf_op | source)
XLA Modules:
  0.0 51.8 jit_solution(14057566438456354878)
XLA Ops:
  0.0 1.2 %shard_map.91 = (f32[16,3712]{1,0:T(8,128)S(1)}, f32[16,3712]{1,0:T(8,128)S(1)}, f32[1,1792]{1,0:T(1,128)S(1)}, f32[1,16]{1,0:T(1,128)S(1)}) custom-call(f32[1,16,7168]{2,1,0:T(8,128)} %refs_0_.1, bf16[4,7168]{1,0:T(4,128)(2,1)} %refs_1_.1, s32[4,8]{1,0:T(4,128)} %refs_2_.1, f32[4,8]{1,0:T(4,128)} %refs_3_.1, f32[56,128]{1,0:T(8,128)} %bitcast.2, ...), custom_call_target="tpu_custom_call" | custom-call | flops 1 | bytes 1 | tf_op jit(solution)/shard_map/pallas_call | solution.py:124
  1.7 1.1 %collective-permute-done.got = f32[16,3712]{1,0:T(8,128)S(1)} collective-permute-done((f32[16,3712]{1,0:T(8,128)S(1)}, f32[16,3712]{1,0:T(8,128)S(1)}, u32[]{:S(2)}, u32[]{:S(2)}) %collective-permute-start) | collective-permute-done | bytes 237600 | tf_op jit(solution)/shard_map/ppermute | solution.py:24
  2.9 2.9 %collective-permute-start.1 = (bf16[16,1920]{1,0:T(8,128)(2,1)S(1)}, bf16[16,1920]{1,0:T(8,128)(2,1)S(1)}, u32[]{:S(2)}, u32[]{:S(2)}) collective-permute-start(bf16[16,1920]{1,0:T(8,128)(2,1)S(1)} %get-tuple-element.45), channel_id=1, source_target_pairs={{0,2},{1,3},{2,0},{3,1},{4,6},{5,7},{6,4},{7,5},{8,10},{9,11},{10,... | collective-permute-start | bytes 184328 | tf_op jit(solution)/shard_map/ppermute | solution.py:24
  5.8 2.3 %collective-permute-done.1.got = bf16[16,1920]{1,0:T(8,128)(2,1)S(1)} collective-permute-done((bf16[16,1920]{1,0:T(8,128)(2,1)S(1)}, bf16[16,1920]{1,0:T(8,128)(2,1)S(1)}, u32[]{:S(2)}, u32[]{:S(2)}) %collective-permute-start.1) | collective-permute-done | bytes 61472 | tf_op jit(solution)/shard_map/ppermute | solution.py:24
  8.3 4.0 %collective-permute-start.4 = (bf16[16,1920]{1,0:T(8,128)(2,1)S(1)}, bf16[16,1920]{1,0:T(8,128)(2,1)S(1)}, u32[]{:S(2)}, u32[]{:S(2)}) collective-permute-start(bf16[16,1920]{1,0:T(8,128)(2,1)S(1)} %shard_map.93.after.s0.stream), channel_id=1, source_target_pairs={{0,12},{4,8},{8,4},{12,0},{1,13},{5,9},{9,5},{13,1},{2,14},{6,10},... | collective-permute-start | bytes 184328 | tf_op jit(solution)/shard_map/ppermute | solution.py:24
  12.9 4.3 %shard_map.94 = (bf16[1792,1024]{1,0:T(8,128)(2,1)S(1)}, bf16[1792,1024]{1,0:T(8,128)(2,1)S(1)}, bf16[1792,1024]{1,0:T(8,128)(2,1)S(1)}, bf16[1792,1024]{1,0:T(8...) custom-call(bf16[1792,4096]{1,0:T(8,128)(2,1)S(1)} %copy-done, ...), custom_call_target="tpu_custom_call" | custom-call | flops 1 | bytes 1 | tf_op jit(solution)/shard_map/pallas_call | solution.py:124
  17.6 1.4 %shard_map.95 = (bf16[64,1792]{1,0:T(8,128)(2,1)S(1)}, bf16[64,2176]{1,0:T(8,128)(2,1)S(1)}, f32[64,128]{1,0:T(8,128)S(1)}, f32[64,128]{1,0:T(8,128)S(1)}) custom-call(bf16[16,1920]{1,0:T(8,128)(2,1)S(1)} %shard_map.93.after.s0.stream, bf16[16,1920]{1,0:T(8,128)(2,1)S(1)} %collective-permute-done.2.s1, bf16[16,1920]{1,0:T(8,128)(2,1)S(1)} %collective-permute-done.3.s2, ...), custom_call_target="tpu_custom_call" | custom-call | flops 1 | bytes 1 | tf_op jit(solution)/shard_map/pallas_call | solution.py:124
  19.1 1.4 %shard_map.97 = bf16[64,2048]{1,0:T(8,128)(2,1)S(1)} custom-call(bf16[64,1792]{1,0:T(8,128)(2,1)S(1)} %get-tuple-element.49.x, bf16[1792,1024]{1,0:T(8,128)(2,1)S(1)} %get-tuple-element.51.w_gate, bf16[1792,1024]{1,0:T(8,128)(2,1)S(1)} %get-tuple-element.52.w_up), custom_call_target="tpu_custom_call" | custom-call | flops 1 | bytes 1 | tf_op jit(solution)/shard_map/pallas_call | solution.py:124
  21.0 1.4 %shard_map.99.keep = f32[64,2048]{1,0:T(8,128)S(1)} custom-call(bf16[64,1792]{1,0:T(8,128)(2,1)S(1)} %get-tuple-element.49.x, bf16[1792,1024]{1,0:T(8,128)(2,1)S(1)} %get-tuple-element.56.w_gate, bf16[1792,1024]{1,0:T(8,128)(2,1)S(1)} %get-tuple-element.57.w_up), custom_call_target="tpu_custom_call" | custom-call | flops 1 | bytes 1 | tf_op jit(solution)/shard_map/pallas_call | solution.py:124
  22.9 1.6 %collective-permute-start.8 = (bf16[48,2176]{1,0:T(8,128)(2,1)S(1)}, bf16[48,2176]{1,0:T(8,128)(2,1)S(1)}, u32[]{:S(2)}, u32[]{:S(2)}) collective-permute-start(bf16[48,2176]{1,0:T(8,128)(2,1)S(1)} %get-tuple-element.60), channel_id=1, source_target_pairs={{0,2},{1,3},{2,0},{3,1},{4,6},{5,7},{6,4},{7,5},{8,10},{9,11},{10,... | collective-permute-start | bytes 626696 | tf_op jit(solution)/shard_map/ppermute | solution.py:24
  24.4 2.3 %shard_map.96.keep = f32[64,2048]{1,0:T(8,128)S(1)} custom-call(bf16[64,1792]{1,0:T(8,128)(2,1)S(1)} %get-tuple-element.49.x, bf16[1792,1024]{1,0:T(8,128)(2,1)S(1)} %get-tuple-element.50.up, bf16[1792,4096]{1,0:T(8,128)(2,1)} %gate_hbm.1), custom_call_target="tpu_custom_call" | custom-call | flops 1 | bytes 1 | tf_op jit(solution)/shard_map/pallas_call | solution.py:124
  27.8 5.3 %shard_map.101 = (bf16[1024,1792]{1,0:T(8,128)(2,1)S(1)}, bf16[1024,1792]{1,0:T(8,128)(2,1)S(1)}, bf16[1024,1792]{1,0:T(8,128)(2,1)S(1)}, bf16[1024,1792]{1,0:T(8,128)(2,1)S(1)}, f32[8,128]{1,0:T(8,128)S(1)}) custom-call(bf16[48,2048]{1,0:T(8,128)(2,1)S(1)} %get-tuple-element.55.after, bf16[4096,1792]{1,0:T(8,128)(2,1)} %w_down.1), custom_call_target="tpu_custom_call" | custom-call | flops 1 | bytes 1 | tf_op jit(solution)/shard_map/pallas_call | solution.py:491
  33.4 0.8 %shard_map.103.after.refs_2_ = f32[64,1792]{1,0:T(8,128)S(1)} custom-call(bf16[64,1024]{1,0:T(8,128)(2,1)S(1)} %shard_map.102.refs_0_, bf16[1024,1792]{1,0:T(8,128)(2,1)S(1)} %get-tuple-element.67.refs_1_), custom_call_target="tpu_custom_call" | custom-call | flops 1 | bytes 1 | tf_op jit(solution)/shard_map/pallas_call | solution.py:124
  35.1 0.7 %shard_map.105.refs_2_ = f32[64,1792]{1,0:T(8,128)S(1)} custom-call(bf16[64,1024]{1,0:T(8,128)(2,1)S(1)} %collective-permute-done.10.refs_0_, bf16[1024,1792]{1,0:T(8,128)(2,1)S(1)} %get-tuple-element.70.refs_1_, f32[64,1792]{1,0:T(8,128)S(1)} %shard_map.103.after.refs_2_), custom_call_target="tpu_custom_call" | custom-call | flops 1 | bytes 1 | tf_op jit(solution)/shard_map/pallas_call | solution.py:124
  35.8 0.7 %shard_map.106.refs_2_ = f32[64,1792]{1,0:T(8,128)S(1)} custom-call(bf16[64,1024]{1,0:T(8,128)(2,1)S(1)} %shard_map.104.refs_0_, bf16[1024,1792]{1,0:T(8,128)(2,1)S(1)} %get-tuple-element.69.refs_1_, f32[64,1792]{1,0:T(8,128)S(1)} %shard_map.105.refs_2_), custom_call_target="tpu_custom_call" | custom-call | flops 1 | bytes 1 | tf_op jit(solution)/shard_map/pallas_call | solution.py:124
  36.6 0.8 %shard_map.107 = (f32[16,1792]{1,0:T(8,128)S(1)}, bf16[16,1792]{1,0:T(8,128)(2,1)S(1)}, bf16[16,1792]{1,0:T(8,128)(2,1)S(1)}, bf16[16,1792]{1,0:T(8,128)(2,1)S(1)}) custom-call(bf16[64,1024]{1,0:T(8,128)(2,1)S(1)} %collective-permute-done.9.refs_0_, bf16[1024,1792]{1,0:T(8,128)(2,1)S(1)} %get-tuple-element.68.refs_1_, f32[64,1792]{1,0:T(8,128)S(1)} %shard_map.106.refs_2_), custom_call_target="tpu_custom_call" | custom-call | flops 1 | bytes 1 | tf_op jit(solution)/shard_map/pallas_call | solution.py:124
  37.4 3.5 %collective-permute-start.11 = (bf16[16,1792]{1,0:T(8,128)(2,1)S(1)}, bf16[16,1792]{1,0:T(8,128)(2,1)S(1)}, u32[]{:S(2)}, u32[]{:S(2)}) collective-permute-start(bf16[16,1792]{1,0:T(8,128)(2,1)S(1)} %get-tuple-element.72), channel_id=1, source_target_pairs={{0,12},{4,8},{8,4},{12,0},{1,13},{5,9},{9,5},{13,1},{2,14},{6,10},... | collective-permute-start | bytes 172040 | tf_op jit(solution)/shard_map/ppermute | solution.py:24
  40.9 0.9 %collective-permute-start.13 = (bf16[16,1792]{1,0:T(8,128)(2,1)S(1)}, bf16[16,1792]{1,0:T(8,128)(2,1)S(1)}, u32[]{:S(2)}, u32[]{:S(2)}) collective-permute-start(bf16[16,1792]{1,0:T(8,128)(2,1)S(1)} %get-tuple-element.74), channel_id=1, source_target_pairs={{0,4},{4,0},{8,12},{12,8},{1,5},{5,1},{9,13},{13,9},{2,6},{6,2},{1... | collective-permute-start | bytes 172040 | tf_op jit(solution)/shard_map/ppermute | solution.py:24
  41.8 2.3 %collective-permute-done.11.r3 = bf16[16,1792]{1,0:T(8,128)(2,1)S(1)} collective-permute-done((bf16[16,1792]{1,0:T(8,128)(2,1)S(1)}, bf16[16,1792]{1,0:T(8,128)(2,1)S(1)}, u32[]{:S(2)}, u32[]{:S(2)}) %collective-permute-start.11) | collective-permute-done | bytes 57376 | tf_op jit(solution)/shard_map/ppermute | solution.py:24
  44.1 1.9 %collective-permute-done.12.r2 = bf16[16,1792]{1,0:T(8,128)(2,1)S(1)} collective-permute-done((bf16[16,1792]{1,0:T(8,128)(2,1)S(1)}, bf16[16,1792]{1,0:T(8,128)(2,1)S(1)}, u32[]{:S(2)}, u32[]{:S(2)}) %collective-permute-start.12) | collective-permute-done | bytes 57376 | tf_op jit(solution)/shard_map/ppermute | solution.py:24
  46.5 1.6 %collective-permute-start.15 = (bf16[4,1792]{1,0:T(4,128)(2,1)S(1)}, bf16[4,1792]{1,0:T(4,128)(2,1)S(1)}, u32[]{:S(2)}, u32[]{:S(2)}) collective-permute-start(bf16[4,1792]{1,0:T(4,128)(2,1)S(1)} %get-tuple-element.77), channel_id=1, source_target_pairs={{0,2},{1,3},{2,0},{3,1},{4,6},{5,7},{6,4},{7,5},{8,10},{9,11},{10,... | collective-permute-start | bytes 43016 | tf_op jit(solution)/shard_map/ppermute | solution.py:24
  48.3 1.9 %collective-permute-done.15.m2 = bf16[4,1792]{1,0:T(4,128)(2,1)S(1)} collective-permute-done((bf16[4,1792]{1,0:T(4,128)(2,1)S(1)}, bf16[4,1792]{1,0:T(4,128)(2,1)S(1)}, u32[]{:S(2)}, u32[]{:S(2)}) %collective-permute-start.15) | collective-permute-done | bytes 14368 | tf_op jit(solution)/shard_map/ppermute | solution.py:24
  50.2 0.9 %collective-permute-done.16.m3 = bf16[4,1792]{1,0:T(4,128)(2,1)S(1)} collective-permute-done((bf16[4,1792]{1,0:T(4,128)(2,1)S(1)}, bf16[4,1792]{1,0:T(4,128)(2,1)S(1)}, u32[]{:S(2)}, u32[]{:S(2)}) %collective-permute-start.16) | collective-permute-done | bytes 14368 | tf_op jit(solution)/shard_map/ppermute | solution.py:24
  51.2 0.7 %shard_map.109 = bf16[4,7168]{1,0:T(4,128)(2,1)} custom-call(bf16[4,1792]{1,0:T(4,128)(2,1)S(1)} %get-tuple-element.75.m0, bf16[4,1792]{1,0:T(4,128)(2,1)S(1)} %collective-permute-done.14.m1, bf16[4,1792]{1,0:T(4,128)(2,1)S(1)} %collective-permute-done.15.m2, bf16[4,1792]{1,0:T(4,128)(2,1)S(1)} %collective-permute-done.16.m3), custom_call_target="tpu_custom_call" | custom-call | flops 1 | bytes 1 | tf_op jit(solution)/shard_map/pallas_call | solution.py:124
  (31 shorter events, 5.7 us)
Async XLA Ops:
  1.2 1.6 %collective-permute-start = (f32[16,3712]{1,0:T(8,128)S(1)}, f32[16,3712]{1,0:T(8,128)S(1)}, u32[]{:S(2)}, u32[]{:S(2)}) collective-permute-start(f32[16,3712]{1,0:T(8,128)S(1)} %get-tuple-element.43), channel_id=1, source_target_pairs={{0,1},{1,0},{2,3},{3,2},{4,5},{5,4},{6,7},{7,6},{8,9},{9,8},{10,11... | collective-permute-start | bytes 712712 | tf_op jit(solution)/shard_map/ppermute | solution.py:24
  2.8 10.1 %copy-start = (bf16[1792,4096]{1,0:T(8,128)(2,1)S(1)}, bf16[1792,4096]{1,0:T(8,128)(2,1)}, u32[]{:S(2)}) copy-start(bf16[1792,4096]{1,0:T(8,128)(2,1)} %w_up.1) | copy-start | bytes 44040196
  2.9 5.2 %collective-permute-start.1 = (bf16[16,1920]{1,0:T(8,128)(2,1)S(1)}, bf16[16,1920]{1,0:T(8,128)(2,1)S(1)}, u32[]{:S(2)}, u32[]{:S(2)}) collective-permute-start(bf16[16,1920]{1,0:T(8,128)(2,1)S(1)} %get-tuple-element.45), channel_id=1, source_target_pairs={{0,2},{1,3},{2,0},{3,1},{4,6},{5,7},{6,4},{7,5},{8,10},{9,11},{10,... | collective-permute-start | bytes 184328 | tf_op jit(solution)/shard_map/ppermute | solution.py:24
  8.3 9.0 %collective-permute-start.4 = (bf16[16,1920]{1,0:T(8,128)(2,1)S(1)}, bf16[16,1920]{1,0:T(8,128)(2,1)S(1)}, u32[]{:S(2)}, u32[]{:S(2)}) collective-permute-start(bf16[16,1920]{1,0:T(8,128)(2,1)S(1)} %shard_map.93.after.s0.stream), channel_id=1, source_target_pairs={{0,12},{4,8},{8,4},{12,0},{1,13},{5,9},{9,5},{13,1},{2,14},{6,10},... | collective-permute-start | bytes 184328 | tf_op jit(solution)/shard_map/ppermute | solution.py:24
  12.3 5.3 %collective-permute-start.3 = (bf16[16,1920]{1,0:T(8,128)(2,1)S(1)}, bf16[16,1920]{1,0:T(8,128)(2,1)S(1)}, u32[]{:S(2)}, u32[]{:S(2)}) collective-permute-start(bf16[16,1920]{1,0:T(8,128)(2,1)S(1)} %shard_map.93.after.s0.stream), channel_id=1, source_target_pairs={{0,8},{4,12},{8,0},{12,4},{1,9},{5,13},{9,1},{13,5},{2,10},{6,14},... | collective-permute-start | bytes 184328 | tf_op jit(solution)/shard_map/ppermute | solution.py:24
  12.3 5.3 %collective-permute-start.2 = (bf16[16,1920]{1,0:T(8,128)(2,1)S(1)}, bf16[16,1920]{1,0:T(8,128)(2,1)S(1)}, u32[]{:S(2)}, u32[]{:S(2)}) collective-permute-start(bf16[16,1920]{1,0:T(8,128)(2,1)S(1)} %shard_map.93.after.s0.stream), channel_id=1, source_target_pairs={{0,4},{4,0},{8,12},{12,8},{1,5},{5,1},{9,13},{13,9},{2,6},{6,2},{1... | collective-permute-start | bytes 184328 | tf_op jit(solution)/shard_map/ppermute | solution.py:24
  19.0 3.5 %collective-permute-start.7 = (bf16[64,2176]{1,0:T(8,128)(2,1)S(1)}, bf16[64,2176]{1,0:T(8,128)(2,1)S(1)}, u32[]{:S(2)}, u32[]{:S(2)}) collective-permute-start(bf16[64,2176]{1,0:T(8,128)(2,1)S(1)} %get-tuple-element.58), channel_id=1, source_target_pairs={{0,1},{1,0},{2,3},{3,2},{4,5},{5,4},{6,7},{7,6},{8,9},{9,8},{10,11... | collective-permute-start | bytes 835592 | tf_op jit(solution)/shard_map/ppermute | solution.py:24
  20.5 6.3 %collective-permute-start.5 = (bf16[64,2048]{1,0:T(8,128)(2,1)S(1)}, bf16[64,2048]{1,0:T(8,128)(2,1)S(1)}, u32[]{:S(2)}, u32[]{:S(2)}) collective-permute-start(bf16[64,2048]{1,0:T(8,128)(2,1)S(1)} %shard_map.97), channel_id=1, source_target_pairs={{0,1},{1,0},{2,3},{3,2},{4,5},{5,4},{6,7},{7,6},{8,9},{9,8},{10,11... | collective-permute-start | bytes 786440 | tf_op jit(solution)/shard_map/ppermute | solution.py:24
  22.9 10.2 %collective-permute-start.8 = (bf16[48,2176]{1,0:T(8,128)(2,1)S(1)}, bf16[48,2176]{1,0:T(8,128)(2,1)S(1)}, u32[]{:S(2)}, u32[]{:S(2)}) collective-permute-start(bf16[48,2176]{1,0:T(8,128)(2,1)S(1)} %get-tuple-element.60), channel_id=1, source_target_pairs={{0,2},{1,3},{2,0},{3,1},{4,6},{5,7},{6,4},{7,5},{8,10},{9,11},{10,... | collective-permute-start | bytes 626696 | tf_op jit(solution)/shard_map/ppermute | solution.py:24
  27.2 7.1 %collective-permute-start.6 = (bf16[48,2048]{1,0:T(8,128)(2,1)S(1)}, bf16[48,2048]{1,0:T(8,128)(2,1)S(1)}, u32[]{:S(2)}, u32[]{:S(2)}) collective-permute-start(bf16[48,2048]{1,0:T(8,128)(2,1)S(1)} %get-tuple-element.55.after), channel_id=1, source_target_pairs={{0,2},{1,3},{2,0},{3,1},{4,6},{5,7},{6,4},{7,5},{8,10},{9,11},{10,... | collective-permute-start | bytes 589832 | tf_op jit(solution)/shard_map/ppermute | solution.py:24
  33.4 1.7 %collective-permute-start.10 = (bf16[64,1024]{1,0:T(8,128)(2,1)S(1)}, bf16[64,1024]{1,0:T(8,128)(2,1)S(1)}, u32[]{:S(2)}, u32[]{:S(2)}) collective-permute-start(bf16[64,1024]{1,0:T(8,128)(2,1)S(1)} %shard_map.102.refs_0_), channel_id=1, source_target_pairs={{0,1},{1,0},{2,3},{3,2},{4,5},{5,4},{6,7},{7,6},{8,9},{9,8},{10,11... | collective-permute-start | bytes 393224 | tf_op jit(solution)/shard_map/ppermute | solution.py:24
  34.5 2.0 %collective-permute-start.9 = (bf16[64,1024]{1,0:T(8,128)(2,1)S(1)}, bf16[64,1024]{1,0:T(8,128)(2,1)S(1)}, u32[]{:S(2)}, u32[]{:S(2)}) collective-permute-start(bf16[64,1024]{1,0:T(8,128)(2,1)S(1)} %shard_map.104.refs_0_), channel_id=1, source_target_pairs={{0,1},{1,0},{2,3},{3,2},{4,5},{5,4},{6,7},{7,6},{8,9},{9,8},{10,11... | collective-permute-start | bytes 393224 | tf_op jit(solution)/shard_map/ppermute | solution.py:24
  37.4 6.7 %collective-permute-start.11 = (bf16[16,1792]{1,0:T(8,128)(2,1)S(1)}, bf16[16,1792]{1,0:T(8,128)(2,1)S(1)}, u32[]{:S(2)}, u32[]{:S(2)}) collective-permute-start(bf16[16,1792]{1,0:T(8,128)(2,1)S(1)} %get-tuple-element.72), channel_id=1, source_target_pairs={{0,12},{4,8},{8,4},{12,0},{1,13},{5,9},{9,5},{13,1},{2,14},{6,10},... | collective-permute-start | bytes 172040 | tf_op jit(solution)/shard_map/ppermute | solution.py:24
  40.9 5.1 %collective-permute-start.12 = (bf16[16,1792]{1,0:T(8,128)(2,1)S(1)}, bf16[16,1792]{1,0:T(8,128)(2,1)S(1)}, u32[]{:S(2)}, u32[]{:S(2)}) collective-permute-start(bf16[16,1792]{1,0:T(8,128)(2,1)S(1)} %get-tuple-element.73), channel_id=1, source_target_pairs={{0,8},{4,12},{8,0},{12,4},{1,9},{5,13},{9,1},{13,5},{2,10},{6,14},... | collective-permute-start | bytes 172040 | tf_op jit(solution)/shard_map/ppermute | solution.py:24
  40.9 5.4 %collective-permute-start.13 = (bf16[16,1792]{1,0:T(8,128)(2,1)S(1)}, bf16[16,1792]{1,0:T(8,128)(2,1)S(1)}, u32[]{:S(2)}, u32[]{:S(2)}) collective-permute-start(bf16[16,1792]{1,0:T(8,128)(2,1)S(1)} %get-tuple-element.74), channel_id=1, source_target_pairs={{0,4},{4,0},{8,12},{12,8},{1,5},{5,1},{9,13},{13,9},{2,6},{6,2},{1... | collective-permute-start | bytes 172040 | tf_op jit(solution)/shard_map/ppermute | solution.py:24
  46.4 1.9 %collective-permute-start.14 = (bf16[4,1792]{1,0:T(4,128)(2,1)S(1)}, bf16[4,1792]{1,0:T(4,128)(2,1)S(1)}, u32[]{:S(2)}, u32[]{:S(2)}) collective-permute-start(bf16[4,1792]{1,0:T(4,128)(2,1)S(1)} %get-tuple-element.76), channel_id=1, source_target_pairs={{0,1},{1,0},{2,3},{3,2},{4,5},{5,4},{6,7},{7,6},{8,9},{9,8},{10,11... | collective-permute-start | bytes 43016 | tf_op jit(solution)/shard_map/ppermute | solution.py:24
  46.5 3.8 %collective-permute-start.15 = (bf16[4,1792]{1,0:T(4,128)(2,1)S(1)}, bf16[4,1792]{1,0:T(4,128)(2,1)S(1)}, u32[]{:S(2)}, u32[]{:S(2)}) collective-permute-start(bf16[4,1792]{1,0:T(4,128)(2,1)S(1)} %get-tuple-element.77), channel_id=1, source_target_pairs={{0,2},{1,3},{2,0},{3,1},{4,6},{5,7},{6,4},{7,5},{8,10},{9,11},{10,... | collective-permute-start | bytes 43016 | tf_op jit(solution)/shard_map/ppermute | solution.py:24
  48.0 3.1 %collective-permute-start.16 = (bf16[4,1792]{1,0:T(4,128)(2,1)S(1)}, bf16[4,1792]{1,0:T(4,128)(2,1)S(1)}, u32[]{:S(2)}, u32[]{:S(2)}) collective-permute-start(bf16[4,1792]{1,0:T(4,128)(2,1)S(1)} %get-tuple-element.78), channel_id=1, source_target_pairs={{0,3},{1,2},{2,1},{3,0},{4,7},{5,6},{6,5},{7,4},{8,11},{9,10},{10,... | collective-permute-start | bytes 43016 | tf_op jit(solution)/shard_map/ppermute | solution.py:24

commit v5 on v4

--- a/solution.py
+++ b/solution.py
@@ -419,7 +419,7 @@
         m[...] = t.astype(bf16)
 
 
-def final_kernel(m0, m1, m2, m3, out):
+def final_kernel(m0, m3, m2, m1, out):
     c = lax.axis_index("cuts")
     part = m0.shape[1]
     p = [m[...].astype(f32) for m in (m0, m1, m2, m3)]
@@ -520,8 +520,8 @@
     )
     r3, r2, r1 = [swap(o, "expert", k) for k, o in ((3, o3), (2, o2), (1, o1))]
     m0, m1, m2, m3 = call(mixed_kernel, [((own_rows, part), bf16)] * 4, s0, o0, r3, r2, r1)
-    m2, m3, m1 = [swap(m, "cuts", k) for k, m in ((2, m2), (3, m3), (1, m1))]
-    (mixed,) = call(final_kernel, [((own_rows, width), bf16)], m0, m1, m2, m3)
+    m3, m2, m1 = [swap(m, "cuts", k) for k, m in ((3, m3), (2, m2), (1, m1))]
+    (mixed,) = call(final_kernel, [((own_rows, width), bf16)], m0, m3, m2, m1)
     return mixed
 
 

time: 52 us -> 51.1 us (0.983)
  waiting for transfers between devices: 11.1 us -> 10.2 us
    ppermute x17, waiting for transfers between devices: 11.1 us -> 10.2 us  [swap(): return lax.ppermute(x, axis, [(i, i ^ bit) for i in range(n)])]
  transfers between devices with their start and end apart: 17 -> 17, of which waited for: 8 -> 8; matrix products, arithmetic and copies ran while one was open for 0% -> 0% of each run, Pallas kernels for 35% -> 36%
where the time goes in v5:
time: 51.1 us; the launch traced here: 50.9 us
  Pallas kernels  22.7 us (44%)
  starting transfers between devices  17.8 us (35%)
  waiting for transfers between devices  10.2 us (20%)
    ppermute x17, starting transfers between devices, swap(): return lax.ppermute(x, axis, [(i, i ^ bit) for i in range(n)])  17.8 us
    pallas_call x18, Pallas kernels, call(): pl.pallas_call(kernel, in_specs=[VM] * (len(args) - far) + [HB] * far, ou...  17.4 us
    ppermute x17, waiting for transfers between devices, swap(): return lax.ppermute(x, axis, [(i, i ^ bit) for i in range(n)])  10.2 us
    pallas_call x1, Pallas kernels, fast_body(): pl.pallas_call(load_down_kernel, in_specs=[HB] * 2, out_specs=[VM] * 5, o...  5.28 us
  transfers between devices with their start and end apart: 17, of which 8 were waited for; matrix products, arithmetic and copies ran while one was open for 0% of the time, Pallas kernels for 36%

profile of v5, /device:TPU:0, one launch (start us, length us, event | category | flops | bytes accessed | tf_op | source)
XLA Modules:
  0.0 50.9 jit_solution(125670111778871398)
XLA Ops:
  0.0 1.2 %shard_map.91 = (f32[16,3712]{1,0:T(8,128)S(1)}, f32[16,3712]{1,0:T(8,128)S(1)}, f32[1,1792]{1,0:T(1,128)S(1)}, f32[1,16]{1,0:T(1,128)S(1)}) custom-call(f32[1,16,7168]{2,1,0:T(8,128)} %refs_0_.1, bf16[4,7168]{1,0:T(4,128)(2,1)} %refs_1_.1, s32[4,8]{1,0:T(4,128)} %refs_2_.1, f32[4,8]{1,0:T(4,128)} %refs_3_.1, f32[56,128]{1,0:T(8,128)} %bitcast.2, ...), custom_call_target="tpu_custom_call" | custom-call | flops 1 | bytes 1 | tf_op jit(solution)/shard_map/pallas_call | solution.py:124
  1.7 1.1 %collective-permute-done.got = f32[16,3712]{1,0:T(8,128)S(1)} collective-permute-done((f32[16,3712]{1,0:T(8,128)S(1)}, f32[16,3712]{1,0:T(8,128)S(1)}, u32[]{:S(2)}, u32[]{:S(2)}) %collective-permute-start) | collective-permute-done | bytes 237600 | tf_op jit(solution)/shard_map/ppermute | solution.py:24
  2.9 2.9 %collective-permute-start.1 = (bf16[16,1920]{1,0:T(8,128)(2,1)S(1)}, bf16[16,1920]{1,0:T(8,128)(2,1)S(1)}, u32[]{:S(2)}, u32[]{:S(2)}) collective-permute-start(bf16[16,1920]{1,0:T(8,128)(2,1)S(1)} %get-tuple-element.45), channel_id=1, source_target_pairs={{0,2},{1,3},{2,0},{3,1},{4,6},{5,7},{6,4},{7,5},{8,10},{9,11},{10,... | collective-permute-start | bytes 184328 | tf_op jit(solution)/shard_map/ppermute | solution.py:24
  5.8 2.3 %collective-permute-done.1.got = bf16[16,1920]{1,0:T(8,128)(2,1)S(1)} collective-permute-done((bf16[16,1920]{1,0:T(8,128)(2,1)S(1)}, bf16[16,1920]{1,0:T(8,128)(2,1)S(1)}, u32[]{:S(2)}, u32[]{:S(2)}) %collective-permute-start.1) | collective-permute-done | bytes 61472 | tf_op jit(solution)/shard_map/ppermute | solution.py:24
  8.3 4.0 %collective-permute-start.4 = (bf16[16,1920]{1,0:T(8,128)(2,1)S(1)}, bf16[16,1920]{1,0:T(8,128)(2,1)S(1)}, u32[]{:S(2)}, u32[]{:S(2)}) collective-permute-start(bf16[16,1920]{1,0:T(8,128)(2,1)S(1)} %shard_map.93.after.s0.stream), channel_id=1, source_target_pairs={{0,12},{4,8},{8,4},{12,0},{1,13},{5,9},{9,5},{13,1},{2,14},{6,10},... | collective-permute-start | bytes 184328 | tf_op jit(solution)/shard_map/ppermute | solution.py:24
  12.3 0.6 %collective-permute-start.2 = (bf16[16,1920]{1,0:T(8,128)(2,1)S(1)}, bf16[16,1920]{1,0:T(8,128)(2,1)S(1)}, u32[]{:S(2)}, u32[]{:S(2)}) collective-permute-start(bf16[16,1920]{1,0:T(8,128)(2,1)S(1)} %shard_map.93.after.s0.stream), channel_id=1, source_target_pairs={{0,4},{4,0},{8,12},{12,8},{1,5},{5,1},{9,13},{13,9},{2,6},{6,2},{1... | collective-permute-start | bytes 184328 | tf_op jit(solution)/shard_map/ppermute | solution.py:24
  12.9 4.3 %shard_map.94 = (bf16[1792,1024]{1,0:T(8,128)(2,1)S(1)}, bf16[1792,1024]{1,0:T(8,128)(2,1)S(1)}, bf16[1792,1024]{1,0:T(8,128)(2,1)S(1)}, bf16[1792,1024]{1,0:T(8...) custom-call(bf16[1792,4096]{1,0:T(8,128)(2,1)S(1)} %copy-done, ...), custom_call_target="tpu_custom_call" | custom-call | flops 1 | bytes 1 | tf_op jit(solution)/shard_map/pallas_call | solution.py:124
  17.6 1.4 %shard_map.95 = (bf16[64,1792]{1,0:T(8,128)(2,1)S(1)}, bf16[64,2176]{1,0:T(8,128)(2,1)S(1)}, f32[64,128]{1,0:T(8,128)S(1)}, f32[64,128]{1,0:T(8,128)S(1)}) custom-call(bf16[16,1920]{1,0:T(8,128)(2,1)S(1)} %shard_map.93.after.s0.stream, bf16[16,1920]{1,0:T(8,128)(2,1)S(1)} %collective-permute-done.2.s1, bf16[16,1920]{1,0:T(8,128)(2,1)S(1)} %collective-permute-done.3.s2, ...), custom_call_target="tpu_custom_call" | custom-call | flops 1 | bytes 1 | tf_op jit(solution)/shard_map/pallas_call | solution.py:124
  19.1 1.4 %shard_map.97 = bf16[64,2048]{1,0:T(8,128)(2,1)S(1)} custom-call(bf16[64,1792]{1,0:T(8,128)(2,1)S(1)} %get-tuple-element.49.x, bf16[1792,1024]{1,0:T(8,128)(2,1)S(1)} %get-tuple-element.51.w_gate, bf16[1792,1024]{1,0:T(8,128)(2,1)S(1)} %get-tuple-element.52.w_up), custom_call_target="tpu_custom_call" | custom-call | flops 1 | bytes 1 | tf_op jit(solution)/shard_map/pallas_call | solution.py:124
  21.0 1.4 %shard_map.99.keep = f32[64,2048]{1,0:T(8,128)S(1)} custom-call(bf16[64,1792]{1,0:T(8,128)(2,1)S(1)} %get-tuple-element.49.x, bf16[1792,1024]{1,0:T(8,128)(2,1)S(1)} %get-tuple-element.56.w_gate, bf16[1792,1024]{1,0:T(8,128)(2,1)S(1)} %get-tuple-element.57.w_up), custom_call_target="tpu_custom_call" | custom-call | flops 1 | bytes 1 | tf_op jit(solution)/shard_map/pallas_call | solution.py:124
  22.9 1.6 %collective-permute-start.8 = (bf16[48,2176]{1,0:T(8,128)(2,1)S(1)}, bf16[48,2176]{1,0:T(8,128)(2,1)S(1)}, u32[]{:S(2)}, u32[]{:S(2)}) collective-permute-start(bf16[48,2176]{1,0:T(8,128)(2,1)S(1)} %get-tuple-element.60), channel_id=1, source_target_pairs={{0,2},{1,3},{2,0},{3,1},{4,6},{5,7},{6,4},{7,5},{8,10},{9,11},{10,... | collective-permute-start | bytes 626696 | tf_op jit(solution)/shard_map/ppermute | solution.py:24
  24.4 2.3 %shard_map.96.keep = f32[64,2048]{1,0:T(8,128)S(1)} custom-call(bf16[64,1792]{1,0:T(8,128)(2,1)S(1)} %get-tuple-element.49.x, bf16[1792,1024]{1,0:T(8,128)(2,1)S(1)} %get-tuple-element.50.up, bf16[1792,4096]{1,0:T(8,128)(2,1)} %gate_hbm.1), custom_call_target="tpu_custom_call" | custom-call | flops 1 | bytes 1 | tf_op jit(solution)/shard_map/pallas_call | solution.py:124
  27.8 5.3 %shard_map.101 = (bf16[1024,1792]{1,0:T(8,128)(2,1)S(1)}, bf16[1024,1792]{1,0:T(8,128)(2,1)S(1)}, bf16[1024,1792]{1,0:T(8,128)(2,1)S(1)}, bf16[1024,1792]{1,0:T(8,128)(2,1)S(1)}, f32[8,128]{1,0:T(8,128)S(1)}) custom-call(bf16[48,2048]{1,0:T(8,128)(2,1)S(1)} %get-tuple-element.55.after, bf16[4096,1792]{1,0:T(8,128)(2,1)} %w_down.1), custom_call_target="tpu_custom_call" | custom-call | flops 1 | bytes 1 | tf_op jit(solution)/shard_map/pallas_call | solution.py:491
  33.4 0.8 %shard_map.103.after.refs_2_ = f32[64,1792]{1,0:T(8,128)S(1)} custom-call(bf16[64,1024]{1,0:T(8,128)(2,1)S(1)} %shard_map.102.refs_0_, bf16[1024,1792]{1,0:T(8,128)(2,1)S(1)} %get-tuple-element.67.refs_1_), custom_call_target="tpu_custom_call" | custom-call | flops 1 | bytes 1 | tf_op jit(solution)/shard_map/pallas_call | solution.py:124
  35.1 0.7 %shard_map.105.refs_2_ = f32[64,1792]{1,0:T(8,128)S(1)} custom-call(bf16[64,1024]{1,0:T(8,128)(2,1)S(1)} %collective-permute-done.10.refs_0_, bf16[1024,1792]{1,0:T(8,128)(2,1)S(1)} %get-tuple-element.70.refs_1_, f32[64,1792]{1,0:T(8,128)S(1)} %shard_map.103.after.refs_2_), custom_call_target="tpu_custom_call" | custom-call | flops 1 | bytes 1 | tf_op jit(solution)/shard_map/pallas_call | solution.py:124
  35.8 0.7 %shard_map.106.refs_2_ = f32[64,1792]{1,0:T(8,128)S(1)} custom-call(bf16[64,1024]{1,0:T(8,128)(2,1)S(1)} %shard_map.104.refs_0_, bf16[1024,1792]{1,0:T(8,128)(2,1)S(1)} %get-tuple-element.69.refs_1_, f32[64,1792]{1,0:T(8,128)S(1)} %shard_map.105.refs_2_), custom_call_target="tpu_custom_call" | custom-call | flops 1 | bytes 1 | tf_op jit(solution)/shard_map/pallas_call | solution.py:124
  36.6 0.8 %shard_map.107 = (f32[16,1792]{1,0:T(8,128)S(1)}, bf16[16,1792]{1,0:T(8,128)(2,1)S(1)}, bf16[16,1792]{1,0:T(8,128)(2,1)S(1)}, bf16[16,1792]{1,0:T(8,128)(2,1)S(1)}) custom-call(bf16[64,1024]{1,0:T(8,128)(2,1)S(1)} %collective-permute-done.9.refs_0_, bf16[1024,1792]{1,0:T(8,128)(2,1)S(1)} %get-tuple-element.68.refs_1_, f32[64,1792]{1,0:T(8,128)S(1)} %shard_map.106.refs_2_), custom_call_target="tpu_custom_call" | custom-call | flops 1 | bytes 1 | tf_op jit(solution)/shard_map/pallas_call | solution.py:124
  37.4 3.5 %collective-permute-start.11 = (bf16[16,1792]{1,0:T(8,128)(2,1)S(1)}, bf16[16,1792]{1,0:T(8,128)(2,1)S(1)}, u32[]{:S(2)}, u32[]{:S(2)}) collective-permute-start(bf16[16,1792]{1,0:T(8,128)(2,1)S(1)} %get-tuple-element.72), channel_id=1, source_target_pairs={{0,12},{4,8},{8,4},{12,0},{1,13},{5,9},{9,5},{13,1},{2,14},{6,10},... | collective-permute-start | bytes 172040 | tf_op jit(solution)/shard_map/ppermute | solution.py:24
  40.9 0.9 %collective-permute-start.13 = (bf16[16,1792]{1,0:T(8,128)(2,1)S(1)}, bf16[16,1792]{1,0:T(8,128)(2,1)S(1)}, u32[]{:S(2)}, u32[]{:S(2)}) collective-permute-start(bf16[16,1792]{1,0:T(8,128)(2,1)S(1)} %get-tuple-element.74), channel_id=1, source_target_pairs={{0,4},{4,0},{8,12},{12,8},{1,5},{5,1},{9,13},{13,9},{2,6},{6,2},{1... | collective-permute-start | bytes 172040 | tf_op jit(solution)/shard_map/ppermute | solution.py:24
  41.8 2.3 %collective-permute-done.11.r3 = bf16[16,1792]{1,0:T(8,128)(2,1)S(1)} collective-permute-done((bf16[16,1792]{1,0:T(8,128)(2,1)S(1)}, bf16[16,1792]{1,0:T(8,128)(2,1)S(1)}, u32[]{:S(2)}, u32[]{:S(2)}) %collective-permute-start.11) | collective-permute-done | bytes 57376 | tf_op jit(solution)/shard_map/ppermute | solution.py:24
  44.1 1.9 %collective-permute-done.12.r2 = bf16[16,1792]{1,0:T(8,128)(2,1)S(1)} collective-permute-done((bf16[16,1792]{1,0:T(8,128)(2,1)S(1)}, bf16[16,1792]{1,0:T(8,128)(2,1)S(1)}, u32[]{:S(2)}, u32[]{:S(2)}) %collective-permute-start.12) | collective-permute-done | bytes 57376 | tf_op jit(solution)/shard_map/ppermute | solution.py:24
  46.5 1.6 %collective-permute-start.15 = (bf16[4,1792]{1,0:T(4,128)(2,1)S(1)}, bf16[4,1792]{1,0:T(4,128)(2,1)S(1)}, u32[]{:S(2)}, u32[]{:S(2)}) collective-permute-start(bf16[4,1792]{1,0:T(4,128)(2,1)S(1)} %get-tuple-element.77), channel_id=1, source_target_pairs={{0,2},{1,3},{2,0},{3,1},{4,6},{5,7},{6,4},{7,5},{8,10},{9,11},{10,... | collective-permute-start | bytes 43016 | tf_op jit(solution)/shard_map/ppermute | solution.py:24
  48.3 1.4 %collective-permute-done.14.m3 = bf16[4,1792]{1,0:T(4,128)(2,1)S(1)} collective-permute-done((bf16[4,1792]{1,0:T(4,128)(2,1)S(1)}, bf16[4,1792]{1,0:T(4,128)(2,1)S(1)}, u32[]{:S(2)}, u32[]{:S(2)}) %collective-permute-start.14) | collective-permute-done | bytes 14368 | tf_op jit(solution)/shard_map/ppermute | solution.py:24
  50.3 0.7 %shard_map.109 = bf16[4,7168]{1,0:T(4,128)(2,1)} custom-call(bf16[4,1792]{1,0:T(4,128)(2,1)S(1)} %get-tuple-element.75.m0, bf16[4,1792]{1,0:T(4,128)(2,1)S(1)} %collective-permute-done.14.m3, bf16[4,1792]{1,0:T(4,128)(2,1)S(1)} %collective-permute-done.15.m2, bf16[4,1792]{1,0:T(4,128)(2,1)S(1)} %collective-permute-done.16.m1), custom_call_target="tpu_custom_call" | custom-call | flops 1 | bytes 1 | tf_op jit(solution)/shard_map/pallas_call | solution.py:124
  (31 shorter events, 5.6 us)
Async XLA Ops:
  1.2 1.6 %collective-permute-start = (f32[16,3712]{1,0:T(8,128)S(1)}, f32[16,3712]{1,0:T(8,128)S(1)}, u32[]{:S(2)}, u32[]{:S(2)}) collective-permute-start(f32[16,3712]{1,0:T(8,128)S(1)} %get-tuple-element.43), channel_id=1, source_target_pairs={{0,1},{1,0},{2,3},{3,2},{4,5},{5,4},{6,7},{7,6},{8,9},{9,8},{10,11... | collective-permute-start | bytes 712712 | tf_op jit(solution)/shard_map/ppermute | solution.py:24
  2.8 10.1 %copy-start = (bf16[1792,4096]{1,0:T(8,128)(2,1)S(1)}, bf16[1792,4096]{1,0:T(8,128)(2,1)}, u32[]{:S(2)}) copy-start(bf16[1792,4096]{1,0:T(8,128)(2,1)} %w_up.1) | copy-start | bytes 44040196
  2.9 5.2 %collective-permute-start.1 = (bf16[16,1920]{1,0:T(8,128)(2,1)S(1)}, bf16[16,1920]{1,0:T(8,128)(2,1)S(1)}, u32[]{:S(2)}, u32[]{:S(2)}) collective-permute-start(bf16[16,1920]{1,0:T(8,128)(2,1)S(1)} %get-tuple-element.45), channel_id=1, source_target_pairs={{0,2},{1,3},{2,0},{3,1},{4,6},{5,7},{6,4},{7,5},{8,10},{9,11},{10,... | collective-permute-start | bytes 184328 | tf_op jit(solution)/shard_map/ppermute | solution.py:24
  8.3 9.0 %collective-permute-start.4 = (bf16[16,1920]{1,0:T(8,128)(2,1)S(1)}, bf16[16,1920]{1,0:T(8,128)(2,1)S(1)}, u32[]{:S(2)}, u32[]{:S(2)}) collective-permute-start(bf16[16,1920]{1,0:T(8,128)(2,1)S(1)} %shard_map.93.after.s0.stream), channel_id=1, source_target_pairs={{0,12},{4,8},{8,4},{12,0},{1,13},{5,9},{9,5},{13,1},{2,14},{6,10},... | collective-permute-start | bytes 184328 | tf_op jit(solution)/shard_map/ppermute | solution.py:24
  12.3 5.3 %collective-permute-start.3 = (bf16[16,1920]{1,0:T(8,128)(2,1)S(1)}, bf16[16,1920]{1,0:T(8,128)(2,1)S(1)}, u32[]{:S(2)}, u32[]{:S(2)}) collective-permute-start(bf16[16,1920]{1,0:T(8,128)(2,1)S(1)} %shard_map.93.after.s0.stream), channel_id=1, source_target_pairs={{0,8},{4,12},{8,0},{12,4},{1,9},{5,13},{9,1},{13,5},{2,10},{6,14},... | collective-permute-start | bytes 184328 | tf_op jit(solution)/shard_map/ppermute | solution.py:24
  12.3 5.3 %collective-permute-start.2 = (bf16[16,1920]{1,0:T(8,128)(2,1)S(1)}, bf16[16,1920]{1,0:T(8,128)(2,1)S(1)}, u32[]{:S(2)}, u32[]{:S(2)}) collective-permute-start(bf16[16,1920]{1,0:T(8,128)(2,1)S(1)} %shard_map.93.after.s0.stream), channel_id=1, source_target_pairs={{0,4},{4,0},{8,12},{12,8},{1,5},{5,1},{9,13},{13,9},{2,6},{6,2},{1... | collective-permute-start | bytes 184328 | tf_op jit(solution)/shard_map/ppermute | solution.py:24
  19.0 3.5 %collective-permute-start.7 = (bf16[64,2176]{1,0:T(8,128)(2,1)S(1)}, bf16[64,2176]{1,0:T(8,128)(2,1)S(1)}, u32[]{:S(2)}, u32[]{:S(2)}) collective-permute-start(bf16[64,2176]{1,0:T(8,128)(2,1)S(1)} %get-tuple-element.58), channel_id=1, source_target_pairs={{0,1},{1,0},{2,3},{3,2},{4,5},{5,4},{6,7},{7,6},{8,9},{9,8},{10,11... | collective-permute-start | bytes 835592 | tf_op jit(solution)/shard_map/ppermute | solution.py:24
  20.5 6.3 %collective-permute-start.5 = (bf16[64,2048]{1,0:T(8,128)(2,1)S(1)}, bf16[64,2048]{1,0:T(8,128)(2,1)S(1)}, u32[]{:S(2)}, u32[]{:S(2)}) collective-permute-start(bf16[64,2048]{1,0:T(8,128)(2,1)S(1)} %shard_map.97), channel_id=1, source_target_pairs={{0,1},{1,0},{2,3},{3,2},{4,5},{5,4},{6,7},{7,6},{8,9},{9,8},{10,11... | collective-permute-start | bytes 786440 | tf_op jit(solution)/shard_map/ppermute | solution.py:24
  22.9 10.2 %collective-permute-start.8 = (bf16[48,2176]{1,0:T(8,128)(2,1)S(1)}, bf16[48,2176]{1,0:T(8,128)(2,1)S(1)}, u32[]{:S(2)}, u32[]{:S(2)}) collective-permute-start(bf16[48,2176]{1,0:T(8,128)(2,1)S(1)} %get-tuple-element.60), channel_id=1, source_target_pairs={{0,2},{1,3},{2,0},{3,1},{4,6},{5,7},{6,4},{7,5},{8,10},{9,11},{10,... | collective-permute-start | bytes 626696 | tf_op jit(solution)/shard_map/ppermute | solution.py:24
  27.2 7.1 %collective-permute-start.6 = (bf16[48,2048]{1,0:T(8,128)(2,1)S(1)}, bf16[48,2048]{1,0:T(8,128)(2,1)S(1)}, u32[]{:S(2)}, u32[]{:S(2)}) collective-permute-start(bf16[48,2048]{1,0:T(8,128)(2,1)S(1)} %get-tuple-element.55.after), channel_id=1, source_target_pairs={{0,2},{1,3},{2,0},{3,1},{4,6},{5,7},{6,4},{7,5},{8,10},{9,11},{10,... | collective-permute-start | bytes 589832 | tf_op jit(solution)/shard_map/ppermute | solution.py:24
  33.4 1.7 %collective-permute-start.10 = (bf16[64,1024]{1,0:T(8,128)(2,1)S(1)}, bf16[64,1024]{1,0:T(8,128)(2,1)S(1)}, u32[]{:S(2)}, u32[]{:S(2)}) collective-permute-start(bf16[64,1024]{1,0:T(8,128)(2,1)S(1)} %shard_map.102.refs_0_), channel_id=1, source_target_pairs={{0,1},{1,0},{2,3},{3,2},{4,5},{5,4},{6,7},{7,6},{8,9},{9,8},{10,11... | collective-permute-start | bytes 393224 | tf_op jit(solution)/shard_map/ppermute | solution.py:24
  34.5 2.0 %collective-permute-start.9 = (bf16[64,1024]{1,0:T(8,128)(2,1)S(1)}, bf16[64,1024]{1,0:T(8,128)(2,1)S(1)}, u32[]{:S(2)}, u32[]{:S(2)}) collective-permute-start(bf16[64,1024]{1,0:T(8,128)(2,1)S(1)} %shard_map.104.refs_0_), channel_id=1, source_target_pairs={{0,1},{1,0},{2,3},{3,2},{4,5},{5,4},{6,7},{7,6},{8,9},{9,8},{10,11... | collective-permute-start | bytes 393224 | tf_op jit(solution)/shard_map/ppermute | solution.py:24
  37.4 6.7 %collective-permute-start.11 = (bf16[16,1792]{1,0:T(8,128)(2,1)S(1)}, bf16[16,1792]{1,0:T(8,128)(2,1)S(1)}, u32[]{:S(2)}, u32[]{:S(2)}) collective-permute-start(bf16[16,1792]{1,0:T(8,128)(2,1)S(1)} %get-tuple-element.72), channel_id=1, source_target_pairs={{0,12},{4,8},{8,4},{12,0},{1,13},{5,9},{9,5},{13,1},{2,14},{6,10},... | collective-permute-start | bytes 172040 | tf_op jit(solution)/shard_map/ppermute | solution.py:24
  40.9 5.1 %collective-permute-start.12 = (bf16[16,1792]{1,0:T(8,128)(2,1)S(1)}, bf16[16,1792]{1,0:T(8,128)(2,1)S(1)}, u32[]{:S(2)}, u32[]{:S(2)}) collective-permute-start(bf16[16,1792]{1,0:T(8,128)(2,1)S(1)} %get-tuple-element.73), channel_id=1, source_target_pairs={{0,8},{4,12},{8,0},{12,4},{1,9},{5,13},{9,1},{13,5},{2,10},{6,14},... | collective-permute-start | bytes 172040 | tf_op jit(solution)/shard_map/ppermute | solution.py:24
  40.9 5.4 %collective-permute-start.13 = (bf16[16,1792]{1,0:T(8,128)(2,1)S(1)}, bf16[16,1792]{1,0:T(8,128)(2,1)S(1)}, u32[]{:S(2)}, u32[]{:S(2)}) collective-permute-start(bf16[16,1792]{1,0:T(8,128)(2,1)S(1)} %get-tuple-element.74), channel_id=1, source_target_pairs={{0,4},{4,0},{8,12},{12,8},{1,5},{5,1},{9,13},{13,9},{2,6},{6,2},{1... | collective-permute-start | bytes 172040 | tf_op jit(solution)/shard_map/ppermute | solution.py:24
  46.4 3.3 %collective-permute-start.14 = (bf16[4,1792]{1,0:T(4,128)(2,1)S(1)}, bf16[4,1792]{1,0:T(4,128)(2,1)S(1)}, u32[]{:S(2)}, u32[]{:S(2)}) collective-permute-start(bf16[4,1792]{1,0:T(4,128)(2,1)S(1)} %get-tuple-element.76), channel_id=1, source_target_pairs={{0,3},{1,2},{2,1},{3,0},{4,7},{5,6},{6,5},{7,4},{8,11},{9,10},{10,... | collective-permute-start | bytes 43016 | tf_op jit(solution)/shard_map/ppermute | solution.py:24
  46.5 3.8 %collective-permute-start.15 = (bf16[4,1792]{1,0:T(4,128)(2,1)S(1)}, bf16[4,1792]{1,0:T(4,128)(2,1)S(1)}, u32[]{:S(2)}, u32[]{:S(2)}) collective-permute-start(bf16[4,1792]{1,0:T(4,128)(2,1)S(1)} %get-tuple-element.77), channel_id=1, source_target_pairs={{0,2},{1,3},{2,0},{3,1},{4,6},{5,7},{6,4},{7,5},{8,10},{9,11},{10,... | collective-permute-start | bytes 43016 | tf_op jit(solution)/shard_map/ppermute | solution.py:24
  48.0 2.2 %collective-permute-start.16 = (bf16[4,1792]{1,0:T(4,128)(2,1)S(1)}, bf16[4,1792]{1,0:T(4,128)(2,1)S(1)}, u32[]{:S(2)}, u32[]{:S(2)}) collective-permute-start(bf16[4,1792]{1,0:T(4,128)(2,1)S(1)} %get-tuple-element.78), channel_id=1, source_target_pairs={{0,1},{1,0},{2,3},{3,2},{4,5},{5,4},{6,7},{7,6},{8,9},{9,8},{10,11... | collective-permute-start | bytes 43016 | tf_op jit(solution)/shard_map/ppermute | solution.py:24
